TPU v7x, 32 devices: a whole 2x2x4 slice. The times are simulated.
32 devices in a mesh: seq: 2 (over x), dp: 16 (over z, y, core).
Axes of the slice: x: 2, y: 2, z: 4, core: 2. Of those that a mesh axis runs over, the one named last changes fastest.
Arguments:
- tokens: bfloat16 [16, 512, 1024], P('dp', 'seq'), may hold values from -6 to 6
- cotangent: bfloat16 [16, 512, 1024], P('dp', 'seq'), may hold values from -6 to 6
- doc_lengths: int32 [16, 4], P('dp'), may hold values from 64 to 320, as said below
- attend_weight: bfloat16 [1024, 3072], P(('seq', 'dp')), may hold values from -0.25 to 0.25
- query_bias: bfloat16 [1024], P(('seq', 'dp')), may hold values from -4 to 4
- value_bias: bfloat16 [1024], P(('seq', 'dp')), may hold values from -3 to 3
- output_weight: bfloat16 [1024, 1024], P(('seq', 'dp')), may hold values from -0.75 to 0.75
- output_bias: bfloat16 [1024], P(('seq', 'dp')), may hold values from -4 to 4
- first_gain: bfloat16 [1024], P(('seq', 'dp')), may hold values from 0.25 to 1.75
- first_shift: bfloat16 [1024], P(('seq', 'dp')), may hold values from -4 to 4
- inner_weight: bfloat16 [1024, 4096], P(('seq', 'dp')), may hold values from -0.1875 to 0.1875
- inner_bias: bfloat16 [4096], P(('seq', 'dp')), may hold values from -4 to 4
- outer_weight: bfloat16 [4096, 1024], P(('seq', 'dp')), may hold values from -0.09375 to 0.09375
- outer_bias: bfloat16 [1024], P(('seq', 'dp')), may hold values from -4 to 4
- second_gain: bfloat16 [1024], P(('seq', 'dp')), may hold values from 0.25 to 1.75
- second_shift: bfloat16 [1024], P(('seq', 'dp')), may hold values from -4 to 4
Outputs:
- layer_output: bfloat16 [16, 512, 1024], P('dp', 'seq')
- input_grad: float32 [16, 512, 1024], P('dp', 'seq')
- attend_weight_grad: float32 [1024, 3072], P(('seq', 'dp'))
- query_bias_grad: float32 [1024], P(('seq', 'dp'))
- value_bias_grad: float32 [1024], P(('seq', 'dp'))
- output_weight_grad: float32 [1024, 1024], P(('seq', 'dp'))
- output_bias_grad: float32 [1024], P(('seq', 'dp'))
- first_gain_grad: float32 [1024], P(('seq', 'dp'))
- first_shift_grad: float32 [1024], P(('seq', 'dp'))
- inner_weight_grad: float32 [1024, 4096], P(('seq', 'dp'))
- inner_bias_grad: float32 [4096], P(('seq', 'dp'))
- outer_weight_grad: float32 [4096, 1024], P(('seq', 'dp'))
- outer_bias_grad: float32 [1024], P(('seq', 'dp'))
- second_gain_grad: float32 [1024], P(('seq', 'dp'))
- second_shift_grad: float32 [1024], P(('seq', 'dp'))
Inputs may be any that keep to these rules, and one draw needn't show every extreme that they name: `doc_lengths`: each row sums to 512; in each row the document at place 1 or 2, drawn per row, starts among the first 256 tokens and ends among the last 256; each of the other three holds 64 to 127 tokens.
All inputs are finite; a program needn't handle non-finite values.
Results may differ from a plain program's by a relative error of at most 0.029.
Values may be sent and summed in bfloat16 or wider, within the bound.
No kernel may reach another device: no remote copies, remote signals or barrier semaphores. Data moves between devices by JAX's collectives and lax.ppermute only.
A program may use at most 192 MiB of HBM per device.

v0:
```python
import functools

import jax
import jax.numpy as jnp
from jax import lax
from jax.experimental import pallas as pl
from jax.experimental.pallas import tpu as pltpu
from jax.sharding import PartitionSpec as P

D = 1024
HEADS = 16
HEAD = 64
GROUP = 256


epsilon = 1e-12
masked_score = -1e30


def norm_forward(value, gain, shift):
    mean_value = jnp.mean(value, axis=-1, keepdims=True)
    center = value - mean_value
    inverse = lax.rsqrt(jnp.mean(center * center, axis=-1, keepdims=True) + epsilon)
    normed = center * inverse
    return (normed * gain + shift, normed, inverse)


def norm_backward(upstream, normed, inverse, gain):
    scaled = upstream * gain
    first_mean = jnp.mean(scaled, axis=-1, keepdims=True)
    second_mean = jnp.mean(scaled * normed, axis=-1, keepdims=True)
    return inverse * (scaled - first_mean - normed * second_mean)


def exact_gelu(value):
    return jax.nn.gelu(value, approximate=False)


def pair_scores(query_pair, key_pair, allowed, factor):
    raw = (
        jnp.einsum("qhd,khd->hqk", query_pair, key_pair, preferred_element_type=jnp.float32)
        * factor
    )
    return jnp.where(allowed[None], raw, masked_score)


def column_pair(matrix, column_start, row_count):
    return lax.dynamic_slice_in_dim(matrix, column_start, 2 * HEAD, 1).reshape(row_count, 2, HEAD)


def general_local(
    tokens,
    cotangent,
    doc_lengths,
    attend_weight,
    query_bias,
    value_bias,
    output_weight,
    output_bias,
    first_gain,
    first_shift,
    inner_weight,
    inner_bias,
    outer_weight,
    outer_bias,
    second_gain,
    second_shift,
):
    (
        attend_mat,
        query_add,
        value_add,
        output_mat,
        output_add,
        first_scale,
        first_offset,
        inner_mat,
        inner_add,
        outer_mat,
        outer_add,
        second_scale,
        second_offset,
    ) = (
        lax.all_gather(attend_weight, ("seq", "dp"), axis=0, tiled=True),
        lax.all_gather(query_bias, ("seq", "dp"), axis=0, tiled=True),
        lax.all_gather(value_bias, ("seq", "dp"), axis=0, tiled=True),
        lax.all_gather(output_weight, ("seq", "dp"), axis=0, tiled=True),
        lax.all_gather(output_bias, ("seq", "dp"), axis=0, tiled=True),
        lax.all_gather(first_gain, ("seq", "dp"), axis=0, tiled=True),
        lax.all_gather(first_shift, ("seq", "dp"), axis=0, tiled=True),
        lax.all_gather(inner_weight, ("seq", "dp"), axis=0, tiled=True),
        lax.all_gather(inner_bias, ("seq", "dp"), axis=0, tiled=True),
        lax.all_gather(outer_weight, ("seq", "dp"), axis=0, tiled=True),
        lax.all_gather(outer_bias, ("seq", "dp"), axis=0, tiled=True),
        lax.all_gather(second_gain, ("seq", "dp"), axis=0, tiled=True),
        lax.all_gather(second_shift, ("seq", "dp"), axis=0, tiled=True),
    )
    token_rows = tokens.reshape(GROUP, D)
    key_total = GROUP * lax.axis_size("seq")
    group_index = lax.axis_index("seq")
    doc_ends = jnp.cumsum(doc_lengths[0])
    positions = lax.iota(jnp.int32, key_total)
    key_docs = jnp.sum((positions[:, None] >= doc_ends[None, :]).astype(jnp.int32), axis=1)
    query_docs = lax.dynamic_slice_in_dim(key_docs, group_index * GROUP, GROUP)
    allowed = query_docs[:, None] == key_docs[None, :]
    factor = HEAD ** (-0.5)
    pair_count = HEADS // 2
    bias_row = jnp.concatenate(
        [query_add.astype(jnp.float32), jnp.zeros((D,), jnp.float32), value_add.astype(jnp.float32)]
    )
    projected = jnp.dot(token_rows, attend_mat, preferred_element_type=jnp.float32) + bias_row
    queries = projected[:, :D].astype(jnp.bfloat16)
    keys_mine = projected[:, D : 2 * D].astype(jnp.bfloat16)
    values_mine = projected[:, 2 * D :].astype(jnp.bfloat16)
    keys_all, values_all = (
        lax.all_gather(keys_mine, "seq", axis=0, tiled=True),
        lax.all_gather(values_mine, "seq", axis=0, tiled=True),
    )

    def forward_pair(pair_index, state_tuple):
        mixed_heads, logsum = state_tuple
        column_start = pair_index * 2 * HEAD
        query_pair = column_pair(queries, column_start, GROUP)
        key_pair = column_pair(keys_all, column_start, key_total)
        value_pair = column_pair(values_all, column_start, key_total)
        scores = pair_scores(query_pair, key_pair, allowed, factor)
        row_peak = jnp.max(scores, axis=-1, keepdims=True)
        expo_terms = jnp.exp(scores - row_peak)
        row_total = jnp.sum(expo_terms, axis=-1, keepdims=True)
        weights = (expo_terms / row_total).astype(jnp.bfloat16)
        result = jnp.einsum(
            "hqk,khd->qhd", weights, value_pair, preferred_element_type=jnp.float32
        ).reshape(GROUP, 2 * HEAD)
        mixed_heads = lax.dynamic_update_slice_in_dim(mixed_heads, result, column_start, 1)
        logsum = lax.dynamic_update_slice_in_dim(
            logsum, row_peak + jnp.log(row_total), pair_index * 2, 0
        )
        return (mixed_heads, logsum)

    mixed_heads, logsum = lax.fori_loop(
        0,
        pair_count,
        forward_pair,
        (jnp.zeros((GROUP, D), jnp.float32), jnp.zeros((HEADS, GROUP, 1), jnp.float32)),
    )
    attended = mixed_heads.astype(jnp.bfloat16)
    branch = jnp.dot(attended, output_mat, preferred_element_type=jnp.float32) + output_add.astype(
        jnp.float32
    )
    first_out, first_normed, first_inverse = norm_forward(
        token_rows.astype(jnp.float32) + branch,
        first_scale.astype(jnp.float32),
        first_offset.astype(jnp.float32),
    )
    first_low = first_out.astype(jnp.bfloat16)
    pre_act = jnp.dot(first_low, inner_mat, preferred_element_type=jnp.float32) + inner_add.astype(
        jnp.float32
    )
    activated = exact_gelu(pre_act).astype(jnp.bfloat16)
    mlp_out = jnp.dot(activated, outer_mat, preferred_element_type=jnp.float32) + outer_add.astype(
        jnp.float32
    )
    second_out, second_normed, second_inverse = norm_forward(
        first_out + mlp_out, second_scale.astype(jnp.float32), second_offset.astype(jnp.float32)
    )
    layer_output = second_out.astype(jnp.bfloat16).reshape(1, GROUP, D)
    (
        attend_mat,
        query_add,
        value_add,
        output_mat,
        output_add,
        first_scale,
        first_offset,
        inner_mat,
        inner_add,
        outer_mat,
        outer_add,
        second_scale,
        second_offset,
    ) = (
        lax.all_gather(attend_weight, ("seq", "dp"), axis=0, tiled=True),
        lax.all_gather(query_bias, ("seq", "dp"), axis=0, tiled=True),
        lax.all_gather(value_bias, ("seq", "dp"), axis=0, tiled=True),
        lax.all_gather(output_weight, ("seq", "dp"), axis=0, tiled=True),
        lax.all_gather(output_bias, ("seq", "dp"), axis=0, tiled=True),
        lax.all_gather(first_gain, ("seq", "dp"), axis=0, tiled=True),
        lax.all_gather(first_shift, ("seq", "dp"), axis=0, tiled=True),
        lax.all_gather(inner_weight, ("seq", "dp"), axis=0, tiled=True),
        lax.all_gather(inner_bias, ("seq", "dp"), axis=0, tiled=True),
        lax.all_gather(outer_weight, ("seq", "dp"), axis=0, tiled=True),
        lax.all_gather(outer_bias, ("seq", "dp"), axis=0, tiled=True),
        lax.all_gather(second_gain, ("seq", "dp"), axis=0, tiled=True),
        lax.all_gather(second_shift, ("seq", "dp"), axis=0, tiled=True),
    )
    upstream = cotangent.reshape(GROUP, D).astype(jnp.float32)
    grad_second_scale = jnp.sum(upstream * second_normed, axis=0)
    grad_second_offset = jnp.sum(upstream, axis=0)
    grad_two = norm_backward(
        upstream, second_normed, second_inverse, second_scale.astype(jnp.float32)
    )
    grad_mlp = grad_two.astype(jnp.bfloat16)
    grad_outer_add = jnp.sum(grad_mlp.astype(jnp.float32), axis=0)
    grad_outer_mat = jnp.einsum(
        "tf,td->fd", activated, grad_mlp, preferred_element_type=jnp.float32
    )
    grad_act = jnp.einsum("td,fd->tf", grad_mlp, outer_mat, preferred_element_type=jnp.float32)
    unused_value, gelu_pull = jax.vjp(exact_gelu, pre_act)
    grad_pre = gelu_pull(grad_act)[0].astype(jnp.bfloat16)
    grad_inner_add = jnp.sum(grad_pre.astype(jnp.float32), axis=0)
    grad_inner_mat = jnp.einsum(
        "td,tf->df", first_low, grad_pre, preferred_element_type=jnp.float32
    )
    grad_first = (
        jnp.einsum("tf,df->td", grad_pre, inner_mat, preferred_element_type=jnp.float32) + grad_two
    )
    grad_first_scale = jnp.sum(grad_first * first_normed, axis=0)
    grad_first_offset = jnp.sum(grad_first, axis=0)
    grad_hidden = norm_backward(
        grad_first, first_normed, first_inverse, first_scale.astype(jnp.float32)
    )
    grad_branch = grad_hidden.astype(jnp.bfloat16)
    grad_output_add = jnp.sum(grad_branch.astype(jnp.float32), axis=0)
    grad_output_mat = jnp.einsum(
        "td,te->de", attended, grad_branch, preferred_element_type=jnp.float32
    )
    grad_attended = jnp.einsum(
        "te,de->td", grad_branch, output_mat, preferred_element_type=jnp.float32
    ).astype(jnp.bfloat16)

    def backward_pair(pair_index, state_tuple):
        grad_queries, grad_keys, grad_values = state_tuple
        column_start = pair_index * 2 * HEAD
        query_pair = column_pair(queries, column_start, GROUP)
        key_pair = column_pair(keys_all, column_start, key_total)
        value_pair = column_pair(values_all, column_start, key_total)
        upstream_pair = column_pair(grad_attended, column_start, GROUP)
        scores = pair_scores(query_pair, key_pair, allowed, factor)
        pair_logsum = lax.dynamic_slice_in_dim(logsum, pair_index * 2, 2, 0)
        pair_probs = jnp.exp(scores - pair_logsum)
        weights = pair_probs.astype(jnp.bfloat16)
        grad_weights = jnp.einsum(
            "qhd,khd->hqk", upstream_pair, value_pair, preferred_element_type=jnp.float32
        )
        row_dot = jnp.sum(grad_weights * pair_probs, axis=-1, keepdims=True)
        grad_scores = (pair_probs * (grad_weights - row_dot)).astype(jnp.bfloat16)
        query_part = (
            jnp.einsum("hqk,khd->qhd", grad_scores, key_pair, preferred_element_type=jnp.float32)
            * factor
        )
        key_part = (
            jnp.einsum("hqk,qhd->khd", grad_scores, query_pair, preferred_element_type=jnp.float32)
            * factor
        )
        value_part = jnp.einsum(
            "hqk,qhd->khd", weights, upstream_pair, preferred_element_type=jnp.float32
        )
        grad_queries = lax.dynamic_update_slice_in_dim(
            grad_queries, query_part.reshape(GROUP, 2 * HEAD), column_start, 1
        )
        grad_keys = lax.dynamic_update_slice_in_dim(
            grad_keys, key_part.reshape(key_total, 2 * HEAD), column_start, 1
        )
        grad_values = lax.dynamic_update_slice_in_dim(
            grad_values, value_part.reshape(key_total, 2 * HEAD), column_start, 1
        )
        return (grad_queries, grad_keys, grad_values)

    grad_queries, grad_keys, grad_values = lax.fori_loop(
        0,
        pair_count,
        backward_pair,
        (
            jnp.zeros((GROUP, D), jnp.float32),
            jnp.zeros((key_total, D), jnp.float32),
            jnp.zeros((key_total, D), jnp.float32),
        ),
    )
    key_share, value_share = (
        lax.psum_scatter(
            grad_keys.astype(jnp.bfloat16), "seq", scatter_dimension=0, tiled=True
        ).astype(jnp.float32),
        lax.psum_scatter(
            grad_values.astype(jnp.bfloat16), "seq", scatter_dimension=0, tiled=True
        ).astype(jnp.float32),
    )
    grad_projected = jnp.concatenate(
        [
            grad_queries.astype(jnp.bfloat16),
            key_share.astype(jnp.bfloat16),
            value_share.astype(jnp.bfloat16),
        ],
        axis=1,
    )
    grad_query_add = jnp.sum(grad_projected[:, :D].astype(jnp.float32), axis=0)
    grad_value_add = jnp.sum(grad_projected[:, 2 * D :].astype(jnp.float32), axis=0)
    grad_attend_mat = jnp.einsum(
        "td,te->de", token_rows, grad_projected, preferred_element_type=jnp.float32
    )
    input_grad = grad_hidden + jnp.einsum(
        "te,de->td", grad_projected, attend_mat, preferred_element_type=jnp.float32
    )
    (
        sum_attend_mat,
        sum_query_add,
        sum_value_add,
        sum_output_mat,
        sum_output_add,
        sum_first_scale,
        sum_first_offset,
        sum_inner_mat,
        sum_inner_add,
        sum_outer_mat,
        sum_outer_add,
        sum_second_scale,
        sum_second_offset,
    ) = (
        lax.psum_scatter(grad_attend_mat, ("seq", "dp"), scatter_dimension=0, tiled=True),
        lax.psum_scatter(grad_query_add, ("seq", "dp"), scatter_dimension=0, tiled=True),
        lax.psum_scatter(grad_value_add, ("seq", "dp"), scatter_dimension=0, tiled=True),
        lax.psum_scatter(grad_output_mat, ("seq", "dp"), scatter_dimension=0, tiled=True),
        lax.psum_scatter(grad_output_add, ("seq", "dp"), scatter_dimension=0, tiled=True),
        lax.psum_scatter(grad_first_scale, ("seq", "dp"), scatter_dimension=0, tiled=True),
        lax.psum_scatter(grad_first_offset, ("seq", "dp"), scatter_dimension=0, tiled=True),
        lax.psum_scatter(grad_inner_mat, ("seq", "dp"), scatter_dimension=0, tiled=True),
        lax.psum_scatter(grad_inner_add, ("seq", "dp"), scatter_dimension=0, tiled=True),
        lax.psum_scatter(grad_outer_mat, ("seq", "dp"), scatter_dimension=0, tiled=True),
        lax.psum_scatter(grad_outer_add, ("seq", "dp"), scatter_dimension=0, tiled=True),
        lax.psum_scatter(grad_second_scale, ("seq", "dp"), scatter_dimension=0, tiled=True),
        lax.psum_scatter(grad_second_offset, ("seq", "dp"), scatter_dimension=0, tiled=True),
    )
    return (
        layer_output,
        input_grad.reshape(1, GROUP, D),
        sum_attend_mat,
        sum_query_add,
        sum_value_add,
        sum_output_mat,
        sum_output_add,
        sum_first_scale,
        sum_first_offset,
        sum_inner_mat,
        sum_inner_add,
        sum_outer_mat,
        sum_outer_add,
        sum_second_scale,
        sum_second_offset,
    )


AXES = ("seq", "dp")
DEVICES = 32
WIDE = ((3, 4, 2, 1), (3, 1, 4, 2))
NARROW = ((3, 2, 1, 4), (3, 2, 1, 4))
HINT = pl.CostEstimate(flops=1, bytes_accessed=1, transcendentals=0)
REMOTE = GROUP - 64
ROWS = GROUP + REMOTE


def swap(value, masks):
    pairs = [(i, i ^ masks[i & 1]) for i in range(DEVICES)]
    return lax.ppermute(value, AXES, pairs)


def sync(movers, *values):
    state, values = lax.optimization_barrier(([mover.data for mover in movers], values))
    for mover, data in zip(movers, state):
        mover.data = data
    return values


def stage_masks(order, stage):
    return (1 << order[0][stage], 1 << order[1][stage])


def chip_mask(bits, place):
    return sum(1 << b for t, b in enumerate(bits) if place >> t & 1)


def join_body(cut, *refs):
    sems = refs[-1]
    ins, outs = refs[: len(refs) - 3], refs[len(refs) - 3 : -1]
    copies = []
    for number, out_ref in enumerate(outs):
        width = out_ref.shape[2]
        for side in range(2):
            source = ins[side] if cut else ins[2 * number + side]
            count = source.shape[0]
            if cut:
                source = source.at[:, :, pl.ds(number * cut, width)]
            target = out_ref.at[pl.ds(side * count, count)]
            copies.append(pltpu.make_async_copy(source, target, sems.at[2 * number + side]))
    for copy in copies:
        copy.start()
    for copy in copies:
        copy.wait()


def join(pieces, cut=0):
    count, rows, columns = pieces[0].shape
    widths = (cut, columns - cut) if cut else (columns, pieces[2].shape[2])
    return pl.pallas_call(
        functools.partial(join_body, cut),
        out_shape=[
            jax.ShapeDtypeStruct((2 * count, rows, width), jnp.bfloat16) for width in widths
        ],
        in_specs=[pl.BlockSpec(memory_space=pl.ANY)] * len(pieces),
        out_specs=[pl.BlockSpec(memory_space=pltpu.VMEM)] * 2,
        scratch_shapes=[pltpu.SemaphoreType.DMA((4,))],
        compiler_params=pltpu.CompilerParams(vmem_limit_bytes=16 * 2**20),
        cost_estimate=HINT,
    )(*pieces)


class Gather:
    def __init__(self, me, weights, cut, extra=()):
        self.me, self.cut, self.data = me, cut, {}
        core = me & 1
        both = []
        for side in (core, 1 - core):
            parts = []
            for weight in weights:
                half = weight.shape[1] // 2
                parts.append(lax.dynamic_slice(weight, (0, side * half), (weight.shape[0], half)))
            parts.extend(extra)
            both.append(parts[0] if len(parts) == 1 else jnp.concatenate(parts, axis=1))
        self.data["mine"] = both[0]
        self.data["arrived"] = swap(both[1], (1, 1))

    def depth(self):
        mine, other = self.data["mine"], self.data["arrived"]
        first = (self.me & 1) == 0
        both = jnp.concatenate([jnp.where(first, mine, other), jnp.where(first, other, mine)])
        both = both[None]
        self.data = {"held": both, "arrived": swap(both, stage_masks(WIDE, 0))}

    def step(self, stage):
        held, arrived = self.data["held"], self.data["arrived"]
        if stage == 1:
            held = join([held, arrived], self.cut)
        else:
            held = join([piece for pair in zip(held, arrived) for piece in pair])
        arrived = [
            swap(piece, stage_masks(order, stage)) for piece, order in zip(held, (WIDE, NARROW))
        ]
        self.data = {"held": held, "arrived": arrived}

    def share(self, name, cuts=(0, 1)):
        shared = self.data.setdefault(name + " core", [None, None])
        for cut in cuts:
            shared[cut] = swap(self.data[name][cut], (1, 1))

    def pieces(self):
        names = ("held", "arrived", "held core", "arrived core")
        return [piece for name in names for piece in self.data[name]]


def gather_matmul_body(routes, count, tile, me_ref, left_ref, *refs):
    piece_refs = refs[:8]
    out_refs, product_ref = refs[8 : 8 + count], refs[8 + count]
    mats, in_sems, out_sems = refs[9 + count : 9 + 2 * count], refs[-2], refs[-1]
    me = me_ref[0]
    rows = piece_refs[0].shape[1]
    copies = []
    for number, piece in enumerate(piece_refs):
        chunk, arrived, side = number % 2, number // 2 % 2, number // 4
        order = (WIDE, NARROW)[chunk]
        base = me ^ side
        core = base & 1
        for sub in range(8):
            place = 8 * arrived + sub
            mask = jnp.where(core == 0, chip_mask(order[0], place), chip_mask(order[1], place))
            chip = (base ^ mask) >> 1
            for start, width, mat, begin in routes(chunk, mats):
                half = mat.shape[1] // 2
                target = mat.at[
                    pl.ds(pl.multiple_of(chip * rows, rows), rows),
                    pl.ds(pl.multiple_of(core * half + begin, 128), width),
                ]
                source = piece.at[sub, :, pl.ds(start, width)]
                copies.append(pltpu.make_async_copy(source, target, in_sems.at[len(copies)]))
    for copy in copies:
        copy.start()
    kept = []
    per_side = len(copies) // 2
    for side in range(2):
        core = (me ^ side) & 1
        for copy in copies[side * per_side : (side + 1) * per_side]:
            copy.wait()
        for number, (mat, out_ref) in enumerate(zip(mats, out_refs)):
            half = mat.shape[1] // 2
            columns = pl.ds(pl.multiple_of(core * half, half), half)
            kept.append(
                pltpu.make_async_copy(
                    mat.at[:, columns], out_ref.at[:, columns], out_sems.at[2 * number + side]
                )
            )
            kept[-1].start()
        half = product_ref.shape[1] // 2

        def step(i, carry):
            columns = pl.ds(pl.multiple_of(core * half + i * tile, tile), tile)
            product_ref[:, columns] = jnp.dot(
                left_ref[...], mats[0][:, columns], preferred_element_type=jnp.float32
            )
            return carry

        lax.fori_loop(0, half // tile, step, 0)
    for copy in kept:
        copy.wait()


def gather_matmul(gather, routes, widths, left):
    pieces = gather.pieces()
    depth = pieces[0].shape[1] * DEVICES // 2
    mats = [(depth, width) for width in widths]
    return pl.pallas_call(
        functools.partial(gather_matmul_body, routes, len(widths), 512),
        out_shape=[jax.ShapeDtypeStruct(mat, jnp.bfloat16) for mat in mats]
        + [jax.ShapeDtypeStruct((left.shape[0], widths[0]), jnp.float32)],
        in_specs=[
            pl.BlockSpec(memory_space=pltpu.SMEM),
            pl.BlockSpec(memory_space=pltpu.VMEM),
        ]
        + [pl.BlockSpec(memory_space=pl.ANY)] * 8,
        out_specs=[pl.BlockSpec(memory_space=pl.ANY)] * len(widths)
        + [pl.BlockSpec(memory_space=pltpu.VMEM)],
        scratch_shapes=[pltpu.VMEM(mat, jnp.bfloat16) for mat in mats]
        + [pltpu.SemaphoreType.DMA((96,)), pltpu.SemaphoreType.DMA((2 * len(widths),))],
        compiler_params=pltpu.CompilerParams(vmem_limit_bytes=40 * 2**20),
        cost_estimate=HINT,
    )(gather.me.reshape(1), left, *pieces)


def whole_routes(cut, chunk, outs):
    half = outs[0].shape[1] // 2
    return ((0, (cut, half - cut)[chunk], outs[0], chunk * cut),)


def first_routes(chunk, outs):
    if chunk == 0:
        return ((0, outs[0].shape[1] // 2, outs[0], 0),)
    half = outs[1].shape[1] // 2
    return ((0, half, outs[1], 0), (half, outs[2].shape[1] // 2, outs[2], 0))


def place_of(bits, shard):
    place = shard & 1
    for t, b in enumerate(bits):
        place = place | ((shard >> b) & 1) << (t + 1)
    return place


def weight_grad_body(chunks, tile, me_ref, left_ref, right_ref, *refs):
    extra_refs = refs[: -2 * len(chunks)]
    outs = refs[-2 * len(chunks) :]
    me = me_ref[0]
    rows = outs[0].shape[1]
    half = right_ref.shape[1] // 2
    per_tile = tile // rows

    def step(i, carry):
        left = left_ref[:, pl.ds(pl.multiple_of(i * tile, tile), tile)].T
        for side in (1, 0):
            base = me ^ side
            core = base & 1
            right = right_ref[:, pl.ds(pl.multiple_of(core * half, half), half)]
            product = jnp.dot(left, right, preferred_element_type=jnp.float32).astype(
                jnp.bfloat16
            )
            for sub in range(per_tile):
                number = i * per_tile + sub
                shard = number ^ base
                for which, (order, begin, width) in enumerate(chunks):
                    place = jnp.where(
                        core == 0, place_of(order[0], shard), place_of(order[1], shard)
                    )
                    out_ref = outs[2 * which + side]
                    out_ref[place, :, :width] = product[
                        sub * rows : (sub + 1) * rows, begin : begin + width
                    ]
                    for extra_ref in extra_refs:
                        out_ref[place, :, width:] = extra_ref[number]
        return carry

    lax.fori_loop(0, left_ref.shape[1] // tile, step, 0, unroll=2)


def weight_grad(left, right, me, chunks, extra=()):
    depth = left.shape[1]
    rows = depth // DEVICES
    more = sum(e.shape[2] for e in extra)
    shapes = [
        jax.ShapeDtypeStruct((DEVICES, rows, width + more), jnp.bfloat16)
        for _, _, width in chunks
        for _ in range(2)
    ]
    outs = pl.pallas_call(
        functools.partial(weight_grad_body, chunks, 256),
        out_shape=shapes,
        in_specs=[pl.BlockSpec(memory_space=pltpu.SMEM)]
        + [pl.BlockSpec(memory_space=pltpu.VMEM)] * (2 + len(extra)),
        out_specs=[pl.BlockSpec(memory_space=pltpu.VMEM)] * len(shapes),
        compiler_params=pltpu.CompilerParams(vmem_limit_bytes=24 * 2**20),
        cost_estimate=HINT,
    )(me.reshape(1), left, right, *extra)
    return [tuple(outs[i : i + 2]) for i in range(0, len(outs), 2)]


def add_low(one, two):
    return (one.astype(jnp.float32) + two.astype(jnp.float32)).astype(jnp.bfloat16)


def halve_body(*refs):
    count = len(refs) // 6
    for which in range(count):
        held_low, held_high, low, high = refs[4 * which : 4 * which + 4]
        keep_ref, send_ref = refs[4 * count + 2 * which : 4 * count + 2 * which + 2]
        send_ref[...] = add_low(held_high[...], high[...])
        keep_ref[...] = add_low(held_low[...], low[...])


def halve(pairs):
    half = pairs[0][0].shape[0] // 2
    block = max(half // 4, 1)
    steps = half // block
    specs, outs, shapes, values = [], [], [], []
    for held, arrived in pairs:
        _, rows, columns = held.shape
        low = pl.BlockSpec((block, rows, columns), lambda i: (i, 0, 0))
        high = pl.BlockSpec((block, rows, columns), lambda i: (steps + i, 0, 0))
        specs += [low, high, low, high]
        outs += [low, low]
        shapes += [jax.ShapeDtypeStruct((half, rows, columns), jnp.bfloat16)] * 2
        values += [held, held, arrived, arrived]
    results = pl.pallas_call(
        halve_body,
        grid=(steps,),
        in_specs=specs,
        out_specs=outs,
        out_shape=shapes,
        compiler_params=pltpu.CompilerParams(vmem_limit_bytes=16 * 2**20),
        cost_estimate=HINT,
    )(*values)
    return results[0::2], results[1::2]


def first_norm_body(
    rows_ref, mixed_ref, matrix_ref, add_ref, gain_ref, shift_ref, low_ref, out_ref, normed_ref, inverse_ref
):
    branch = jnp.dot(mixed_ref[...], matrix_ref[...], preferred_element_type=jnp.float32)
    out, normed, inverse = norm_forward(
        rows_ref[...].astype(jnp.float32) + (branch + add_ref[...]), gain_ref[...], shift_ref[...]
    )
    low_ref[...] = out.astype(jnp.bfloat16)
    out_ref[...] = out
    normed_ref[...] = normed
    inverse_ref[...] = inverse


def first_norm(rows, mixed, matrix, add, gain, shift):
    block = 128
    tall = pl.BlockSpec((block, D), lambda i: (i, 0))
    whole = pl.BlockSpec((1, D), lambda i: (0, 0))
    return pl.pallas_call(
        first_norm_body,
        grid=(GROUP // block,),
        in_specs=[tall, tall, pl.BlockSpec((D, D), lambda i: (0, 0)), whole, whole, whole],
        out_specs=[tall, tall, tall, pl.BlockSpec((block, 1), lambda i: (i, 0))],
        out_shape=[
            jax.ShapeDtypeStruct((GROUP, D), jnp.bfloat16),
            jax.ShapeDtypeStruct((GROUP, D), jnp.float32),
            jax.ShapeDtypeStruct((GROUP, D), jnp.float32),
            jax.ShapeDtypeStruct((GROUP, 1), jnp.float32),
        ],
        compiler_params=pltpu.CompilerParams(vmem_limit_bytes=20 * 2**20),
        cost_estimate=HINT,
    )(rows, mixed, matrix, add, gain, shift)


def rows_back_body(grad_ref, matrix_ref, near_ref, far_ref):
    product = lax.dot_general(
        grad_ref[...],
        matrix_ref[...],
        (((1,), (1,)), ((), ())),
        preferred_element_type=jnp.float32,
    )
    near_ref[...] = product[:GROUP]
    far_ref[...] = product[GROUP:].astype(jnp.bfloat16)


def rows_back(grad, matrix):
    return pl.pallas_call(
        rows_back_body,
        grid=(4,),
        in_specs=[
            pl.BlockSpec((ROWS, 3 * D), lambda i: (0, 0)),
            pl.BlockSpec((D // 4, 3 * D), lambda i: (i, 0)),
        ],
        out_specs=[
            pl.BlockSpec((GROUP, D // 4), lambda i: (0, i)),
            pl.BlockSpec((REMOTE, D // 4), lambda i: (0, i)),
        ],
        out_shape=[
            jax.ShapeDtypeStruct((GROUP, D), jnp.float32),
            jax.ShapeDtypeStruct((REMOTE, D), jnp.bfloat16),
        ],
        compiler_params=pltpu.CompilerParams(vmem_limit_bytes=16 * 2**20),
        cost_estimate=HINT,
    )(grad, matrix)


def cut_grads(me, left, right, cut):
    half = right.shape[1] // 2
    return weight_grad(left, right, me, ((WIDE, 0, cut), (NARROW, cut, half - cut)))


class Scatter:
    def __init__(self, me, grads):
        self.me, self.stage = me, 4
        self.data = {"held": [keep for keep, _ in grads], "send": [send for _, send in grads]}

    def begin(self):
        self.data["arrived"] = [swap(piece, (1, 1)) for piece in self.data.pop("send")]

    def step(self):
        self.stage -= 1
        held, send = halve(list(zip(self.data["held"], self.data["arrived"])))
        if self.stage == 0:
            held, send = jnp.concatenate(held, axis=2), jnp.concatenate(send, axis=2)
            arrived = swap(send, stage_masks(WIDE, 0))
        else:
            arrived = [
                swap(piece, stage_masks(order, self.stage))
                for piece, order in zip(send, (WIDE, NARROW))
            ]
        self.data = {"held": held, "arrived": arrived}

    def near(self):
        held, arrived = self.data["held"], self.data["arrived"]
        send = add_low(held[1], arrived[1])
        held = held[0].astype(jnp.float32) + arrived[0].astype(jnp.float32)
        self.data = {"held": held, "arrived": swap(send, (1, 1))}

    def result(self):
        held, arrived = self.data["held"], self.data["arrived"].astype(jnp.float32)
        first = (self.me & 1) == 0
        return jnp.where(first, held, arrived), jnp.where(first, arrived, held)


def masked_pair(keys):
    first = lax.broadcasted_iota(jnp.int32, keys.shape, 1) < HEAD
    zeros = jnp.zeros_like(keys)
    return jnp.where(first, keys, zeros), jnp.where(first, zeros, keys)


PAIRS = 2
WIDTH = PAIRS * 128
STEPS = D // WIDTH


def attend_forward_body(query_docs, key_docs, query_ref, key_ref, value_ref, mixed_ref, log_ref):
    allowed = key_docs[...] == query_docs[...]
    for pair in range(PAIRS):
        columns = slice(pair * 128, (pair + 1) * 128)
        queries = query_ref[:, columns]
        value_rows = value_ref[:, columns].T
        results = []
        for head, keys in enumerate(masked_pair(key_ref[:, columns])):
            raw = lax.dot_general(
                keys, queries, (((1,), (1,)), ((), ())), preferred_element_type=jnp.float32
            )
            scores = jnp.where(allowed, raw * HEAD**-0.5, masked_score)
            peak = jnp.max(scores, axis=0, keepdims=True)
            terms = jnp.exp(scores - peak)
            total = jnp.sum(terms, axis=0, keepdims=True)
            weights = (terms * (1.0 / total)).astype(jnp.bfloat16)
            results.append(
                jnp.dot(
                    value_rows[head * HEAD : (head + 1) * HEAD],
                    weights,
                    preferred_element_type=jnp.float32,
                )
            )
            log_ref[pair, head : head + 1] = peak + jnp.log(total)
        mixed_ref[:, columns] = jnp.concatenate(results).T.astype(jnp.bfloat16)


def attend_specs():
    return [
        pl.BlockSpec((1, GROUP), lambda i: (0, 0)),
        pl.BlockSpec((ROWS, 1), lambda i: (0, 0)),
        pl.BlockSpec((GROUP, WIDTH), lambda i: (0, i)),
        pl.BlockSpec((ROWS, WIDTH), lambda i: (0, STEPS + i)),
        pl.BlockSpec((ROWS, WIDTH), lambda i: (0, 2 * STEPS + i)),
    ]


def attend_forward(query_docs, key_docs, projected):
    return pl.pallas_call(
        attend_forward_body,
        grid=(STEPS,),
        in_specs=attend_specs(),
        out_specs=[
            pl.BlockSpec((GROUP, WIDTH), lambda i: (0, i)),
            pl.BlockSpec((PAIRS, 2, GROUP), lambda i: (i, 0, 0)),
        ],
        out_shape=[
            jax.ShapeDtypeStruct((GROUP, D), jnp.bfloat16),
            jax.ShapeDtypeStruct((HEADS // 2, 2, GROUP), jnp.float32),
        ],
        compiler_params=pltpu.CompilerParams(vmem_limit_bytes=16 * 2**20),
        cost_estimate=HINT,
    )(query_docs, key_docs, projected, projected, projected)


def attend_backward_body(
    query_docs, key_docs, query_ref, key_ref, value_ref, upstream_ref, log_ref, grad_ref, sum_ref
):
    allowed = key_docs[...] == query_docs[...]
    across = (((1,), (1,)), ((), ()))
    wide = lax.broadcasted_iota(jnp.int32, (ROWS, 128), 1) < HEAD
    for pair in range(PAIRS):
        columns = slice(pair * 128, (pair + 1) * 128)
        queries, upstream = query_ref[:, columns], upstream_ref[:, columns]
        key_rows = key_ref[:, columns].T
        pairs = zip(masked_pair(key_ref[:, columns]), masked_pair(value_ref[:, columns]))
        query_parts, key_parts, value_parts = [], [], []
        for head, (keys, values) in enumerate(pairs):
            raw = lax.dot_general(keys, queries, across, preferred_element_type=jnp.float32)
            scores = jnp.where(allowed, raw * HEAD**-0.5, masked_score)
            probs = jnp.exp(scores - log_ref[pair, head : head + 1])
            grad_weights = lax.dot_general(
                values, upstream, across, preferred_element_type=jnp.float32
            )
            row_dot = jnp.sum(grad_weights * probs, axis=0, keepdims=True)
            grad_scores = (probs * (grad_weights - row_dot)).astype(jnp.bfloat16)
            weights = probs.astype(jnp.bfloat16)
            query_parts.append(
                jnp.dot(
                    key_rows[head * HEAD : (head + 1) * HEAD],
                    grad_scores,
                    preferred_element_type=jnp.float32,
                )
            )
            key_parts.append(jnp.dot(grad_scores, queries, preferred_element_type=jnp.float32))
            value_parts.append(jnp.dot(weights, upstream, preferred_element_type=jnp.float32))
        grad_queries = (jnp.concatenate(query_parts).T * HEAD**-0.5).astype(jnp.bfloat16)
        grad_keys = jnp.where(wide, key_parts[0], key_parts[1]) * HEAD**-0.5
        grad_values = jnp.where(wide, value_parts[0], value_parts[1]).astype(jnp.bfloat16)
        start = pl.program_id(0) * WIDTH + pair * 128
        query_at, key_at, value_at = (
            pl.ds(pl.multiple_of(start + part * D, 128), 128) for part in range(3)
        )
        grad_ref[:GROUP, query_at] = grad_queries
        grad_ref[GROUP:, query_at] = jnp.zeros((REMOTE, 128), jnp.bfloat16)
        grad_ref[:, key_at] = grad_keys.astype(jnp.bfloat16)
        grad_ref[:, value_at] = grad_values
        low = grad_queries.astype(jnp.float32)
        sum_ref[0, :, query_at] = jnp.sum(low, axis=0, keepdims=True)
        low = grad_values.astype(jnp.float32)
        sum_ref[1, :, query_at] = jnp.sum(low, axis=0, keepdims=True)


def attend_backward(query_docs, key_docs, projected, upstream, logs):
    return pl.pallas_call(
        attend_backward_body,
        grid=(STEPS,),
        in_specs=attend_specs()
        + [
            pl.BlockSpec((GROUP, WIDTH), lambda i: (0, i)),
            pl.BlockSpec((PAIRS, 2, GROUP), lambda i: (i, 0, 0)),
        ],
        out_specs=[
            pl.BlockSpec((ROWS, 3 * D), lambda i: (0, 0)),
            pl.BlockSpec((2, 1, D), lambda i: (0, 0, 0)),
        ],
        out_shape=[
            jax.ShapeDtypeStruct((ROWS, 3 * D), jnp.bfloat16),
            jax.ShapeDtypeStruct((2, 1, D), jnp.float32),
        ],
        compiler_params=pltpu.CompilerParams(vmem_limit_bytes=16 * 2**20),
        cost_estimate=HINT,
    )(query_docs, key_docs, projected, projected, projected, upstream, logs)


def pack_shard(vectors):
    rows = jnp.concatenate([vector.reshape(-1, 32) for vector in vectors])
    return jnp.pad(rows, ((0, 32 - rows.shape[0]), (0, 96)))


def unpack_shards(packed):
    rows = packed.reshape(DEVICES, 32, 256)[:, :12, :32].astype(jnp.float32)
    short = rows[:, :8].transpose(1, 0, 2).reshape(8, 1, D)
    return [short[i] for i in range(8)] + [rows[:, 8:].reshape(1, 4 * D)]


def pack_grads(short, long):
    rows = jnp.concatenate([vector.reshape(1, 8, 128) for vector in short])
    rows = jnp.repeat(rows.transpose(1, 0, 2), 4, axis=0)
    rows = jnp.concatenate([rows, long.reshape(DEVICES, 1, 128)], axis=1)
    return jnp.pad(rows, ((0, 0), (0, 23), (0, 0))).astype(jnp.bfloat16)


def fast_local(
    tokens,
    cotangent,
    doc_lengths,
    attend_weight,
    query_bias,
    value_bias,
    output_weight,
    output_bias,
    first_gain,
    first_shift,
    inner_weight,
    inner_bias,
    outer_weight,
    outer_bias,
    second_gain,
    second_shift,
):
    me = lax.axis_index(AXES)
    group_index = me >> 4
    small_shard = pack_shard(
        [
            query_bias,
            value_bias,
            output_bias,
            first_gain,
            first_shift,
            outer_bias,
            second_gain,
            second_shift,
            inner_bias,
        ]
    )
    attend_cut, inner_cut, outer_cut = 3 * D // 2, 1408, 384
    one = Gather(me, (attend_weight, output_weight), attend_cut, (small_shard,))
    sync((one,))

    one.depth()
    two = Gather(me, (inner_weight,), inner_cut)
    three = Gather(me, (outer_weight,), outer_cut)
    movers = (one, two, three)
    doc_ends = jnp.cumsum(doc_lengths[0])
    near_at = group_index * GROUP + lax.iota(jnp.int32, GROUP)
    far_at = jnp.where(group_index == 0, GROUP, 64) + lax.iota(jnp.int32, REMOTE)
    row_at = jnp.concatenate([near_at, far_at])
    row_docs = jnp.sum((row_at[:, None] >= doc_ends[None, :]).astype(jnp.int32), axis=1)
    query_docs, key_docs = row_docs[None, :GROUP], row_docs[:, None]
    near = tokens.reshape(GROUP, D)
    query_docs, key_docs, near = sync(movers, query_docs, key_docs, near)

    one.step(1)
    two.depth()
    far = lax.dynamic_slice(near, (64 * (1 - group_index), 0), (REMOTE, D))
    far = lax.ppermute(far, "seq", [(0, 1), (1, 0)])
    (far,) = sync((one, two), far)

    one.step(2)
    token_rows = jnp.concatenate([near, far])
    (token_rows,) = sync((one, two), token_rows)

    one.step(3)
    two.step(1)
    three.depth()
    sync(movers)

    one.share("held")
    one.share("arrived")
    sync((one,))

    two.step(2)
    three.step(1)
    attend_mat, output_mat, small_all, projected = gather_matmul(
        one, first_routes, (3 * D, D, 256), token_rows
    )
    (
        query_add,
        value_add,
        output_add,
        first_scale,
        first_offset,
        outer_add,
        second_scale,
        second_offset,
        inner_add,
    ) = unpack_shards(small_all)
    bias_row = jnp.concatenate([query_add, jnp.zeros((1, D), jnp.float32), value_add], axis=1)
    projected = (projected + bias_row).astype(jnp.bfloat16)
    (projected,) = sync((two, three), projected)

    two.step(3)
    two.share("held", (0,))
    three.step(2)
    attended, logs = attend_forward(query_docs, key_docs, projected)
    first_low, first_out, first_normed, first_inverse = first_norm(
        near, attended, output_mat, output_add, first_scale, first_offset
    )
    first_out, first_normed, first_inverse, first_low = sync(
        (two, three), first_out, first_normed, first_inverse, first_low
    )

    two.share("held", (1,))
    two.share("arrived")
    sync((two,))

    three.step(3)
    three.share("held")
    inner_mat, pre_act = gather_matmul(
        two, functools.partial(whole_routes, inner_cut), (4 * D,), first_low
    )
    pre_act = pre_act + inner_add
    cdf = 0.5 * (1.0 + lax.erf(pre_act * 0.5**0.5))
    gelu_slope = cdf + pre_act * jnp.exp(-0.5 * pre_act * pre_act) * 0.3989422804014327
    activated = (pre_act * cdf).astype(jnp.bfloat16)
    activated, gelu_slope = sync((three,), activated, gelu_slope)

    three.share("arrived")
    outer_mat, mlp_out = gather_matmul(
        three, functools.partial(whole_routes, outer_cut), (D,), activated
    )
    mlp_out = mlp_out + outer_add
    second_out, second_normed, second_inverse = norm_forward(
        first_out + mlp_out, second_scale, second_offset
    )
    layer_output = second_out.astype(jnp.bfloat16).reshape(1, GROUP, D)
    upstream = cotangent.reshape(GROUP, D).astype(jnp.float32)
    grad_two = norm_backward(upstream, second_normed, second_inverse, second_scale)
    grad_mlp = grad_two.astype(jnp.bfloat16)
    outer = Scatter(me, cut_grads(me, activated, grad_mlp, outer_cut))
    grad_mlp, grad_two, second_normed = sync((outer,), grad_mlp, grad_two, second_normed)

    outer.begin()
    grad_act = jnp.einsum("td,fd->tf", grad_mlp, outer_mat, preferred_element_type=jnp.float32)
    grad_pre = (grad_act * gelu_slope).astype(jnp.bfloat16)
    inner_sum = jnp.sum(grad_pre.astype(jnp.float32), axis=0)
    grad_pre, inner_sum, grad_mlp, second_normed = sync(
        (outer,), grad_pre, inner_sum, grad_mlp, second_normed
    )

    outer.step()
    inner = Scatter(me, cut_grads(me, first_low, grad_pre, inner_cut))
    second_sums = (
        jnp.sum(grad_mlp.astype(jnp.float32), axis=0),
        jnp.sum(upstream * second_normed, axis=0),
        jnp.sum(upstream, axis=0),
    )
    grad_first = (
        jnp.einsum("tf,df->td", grad_pre, inner_mat, preferred_element_type=jnp.float32) + grad_two
    )
    grad_hidden = norm_backward(grad_first, first_normed, first_inverse, first_scale)
    grad_branch = grad_hidden.astype(jnp.bfloat16)
    first_sums = (
        jnp.sum(grad_branch.astype(jnp.float32), axis=0),
        jnp.sum(grad_first * first_normed, axis=0),
        jnp.sum(grad_first, axis=0),
    )
    grad_attended = jnp.einsum(
        "te,de->td", grad_branch, output_mat, preferred_element_type=jnp.float32
    ).astype(jnp.bfloat16)
    first_sums, second_sums, grad_hidden, grad_branch, grad_attended = sync(
        (outer, inner), first_sums, second_sums, grad_hidden, grad_branch, grad_attended
    )

    inner.begin()
    outer.step()
    grad_projected, row_sums = attend_backward(
        query_docs, key_docs, projected, grad_attended, logs
    )
    grad_projected, row_sums = sync((outer, inner), grad_projected, row_sums)

    inner.step()
    outer.step()
    small = pack_grads([row_sums[0, 0], row_sums[1, 0], *first_sums, *second_sums], inner_sum)
    first = Scatter(
        me,
        weight_grad(token_rows, grad_projected, me, ((WIDE, 0, attend_cut),))
        + weight_grad(attended, grad_branch, me, ((NARROW, 0, D // 2),), (small,)),
    )
    movers = (outer, inner, first)
    sync(movers)

    first.begin()
    inner.step()
    outer.step()
    row_grad, far_grad = rows_back(grad_projected, attend_mat)
    row_grad, far_grad = sync(movers, row_grad, far_grad)

    first.step()
    inner.step()
    outer.near()
    sync(movers)

    first.step()
    inner.step()
    sum_outer_mat = jnp.concatenate(outer.result(), axis=1)
    (sum_outer_mat,) = sync((inner, first), sum_outer_mat)

    first.step()
    inner.near()
    (far_grad,) = sync((inner, first), far_grad)

    first.step()
    far_grad = lax.ppermute(far_grad, "seq", [(0, 1), (1, 0)])
    sum_inner_mat = jnp.concatenate(inner.result(), axis=1)
    sum_inner_mat, far_grad = sync((first,), sum_inner_mat, far_grad)

    first.near()
    filler = jnp.zeros((64, D), jnp.float32)
    far_grad = far_grad.astype(jnp.float32)
    far_grad = jnp.where(
        group_index == 0,
        jnp.concatenate([filler, far_grad]),
        jnp.concatenate([far_grad, filler]),
    )
    input_grad = grad_hidden + row_grad + far_grad
    halves = first.result()
    output_end = attend_cut + D // 2
    sum_attend_mat = jnp.concatenate([half[:, :attend_cut] for half in halves], axis=1)
    sum_output_mat = jnp.concatenate([half[:, attend_cut:output_end] for half in halves], axis=1)
    small_rows = halves[0][:, output_end:]
    own = lax.dynamic_slice(small_rows, (0, 32 * (me & 3)), (8, 32))
    (
        sum_query_add,
        sum_value_add,
        sum_output_add,
        sum_first_scale,
        sum_first_offset,
        sum_outer_add,
        sum_second_scale,
        sum_second_offset,
    ) = (own[i] for i in range(8))
    sum_inner_add = small_rows[8]
    return (
        layer_output,
        input_grad.reshape(1, GROUP, D),
        sum_attend_mat,
        sum_query_add,
        sum_value_add,
        sum_output_mat,
        sum_output_add,
        sum_first_scale,
        sum_first_offset,
        sum_inner_mat,
        sum_inner_add,
        sum_outer_mat,
        sum_outer_add,
        sum_second_scale,
        sum_second_offset,
    )


def solution(mesh):
    sizes = (mesh.shape["seq"], mesh.shape["dp"])
    return jax.shard_map(
        fast_local if sizes == (2, 16) else general_local,
        mesh=mesh,
        in_specs=(
            P("dp", "seq", None),
            P("dp", "seq", None),
            P("dp", None),
            P(("seq", "dp"), None),
            P(("seq", "dp")),
            P(("seq", "dp")),
            P(("seq", "dp"), None),
            P(("seq", "dp")),
            P(("seq", "dp")),
            P(("seq", "dp")),
            P(("seq", "dp"), None),
            P(("seq", "dp")),
            P(("seq", "dp"), None),
            P(("seq", "dp")),
            P(("seq", "dp")),
            P(("seq", "dp")),
        ),
        out_specs=(
            P("dp", "seq", None),
            P("dp", "seq", None),
            P(("seq", "dp"), None),
            P(("seq", "dp")),
            P(("seq", "dp")),
            P(("seq", "dp"), None),
            P(("seq", "dp")),
            P(("seq", "dp")),
            P(("seq", "dp")),
            P(("seq", "dp"), None),
            P(("seq", "dp")),
            P(("seq", "dp"), None),
            P(("seq", "dp")),
            P(("seq", "dp")),
            P(("seq", "dp")),
        ),
        check_vma=False,
    )
```

profile of v0, /device:TPU:1, one launch (start us, length us, event | category | flops | bytes accessed | tf_op | source)
XLA Modules:
  0.0 344.1 jit_solution(8087960064669259928)
XLA Ops:
  6.9 3.8 %collective-permute-start.1 = (bf16[1,64,2176]{2,1,0:T(8,128)(2,1)S(1)}, bf16[1,64,2176]{2,1,0:T(8,128)(2,1)S(1)}, u32[]{:S(2)}, u32[]{:S(2)}) collective-permute-start(bf16[1,64,2176]{2,1,0:T(8,128)(2,1)S(1)} %maximum_bitcast_fusion.refs_0_), channel_id=1, source_target_pairs={{0,8},{1,9},{2,10},{3,11},{4,12},{5,13},{6,14},{7,15},{8,0},{9,1},... | collective-permute-start | bytes 835592 | tf_op jit(solution)/shard_map/ppermute | solution.py:362
  11.0 12.6 %collective-permute-done.1.refs_1_ = bf16[1,64,2176]{2,1,0:T(8,128)(2,1)S(1)} collective-permute-done((bf16[1,64,2176]{2,1,0:T(8,128)(2,1)S(1)}, bf16[1,64,2176]{2,1,0:T(8,128)(2,1)S(1)}, u32[]{:S(2)}, u32[]{:S(2)}) %collective-permute-start.1) | collective-permute-done | bytes 278560 | tf_op jit(solution)/shard_map/ppermute | solution.py:362
  24.9 1.3 collective-permute-start.4
  26.4 3.9 %collective-permute-start.5 = (bf16[2,64,640]{2,1,0:T(8,128)(2,1)S(1)}, bf16[2,64,640]{2,1,0:T(8,128)(2,1)S(1)}, u32[]{:S(2)}, u32[]{:S(2)}) collective-permute-start(bf16[2,64,640]{2,1,0:T(8,128)(2,1)S(1)} %get-tuple-element.297.refs_2_), channel_id=1, source_target_pairs={{0,4},{1,5},{2,6},{3,7},{4,0},{5,1},{6,2},{7,3},{8,12},{9,13},{10,... | collective-permute-start | bytes 491528 | tf_op jit(solution)/shard_map/ppermute | solution.py:362
  30.2 5.3 %collective-permute-done.5.refs_3_ = bf16[2,64,640]{2,1,0:T(8,128)(2,1)S(1)} collective-permute-done((bf16[2,64,640]{2,1,0:T(8,128)(2,1)S(1)}, bf16[2,64,640]{2,1,0:T(8,128)(2,1)S(1)}, u32[]{:S(2)}, u32[]{:S(2)}) %collective-permute-start.5) | collective-permute-done | bytes 163872 | tf_op jit(solution)/shard_map/ppermute | solution.py:362
  35.6 4.8 %collective-permute-done.6.refs_1_ = bf16[1,64,2048]{2,1,0:T(8,128)(2,1)S(1)} collective-permute-done((bf16[1,64,2048]{2,1,0:T(8,128)(2,1)S(1)}, bf16[1,64,2048]{2,1,0:T(8,128)(2,1)S(1)}, u32[]{:S(2)}, u32[]{:S(2)}) %collective-permute-start.6) | collective-permute-done | bytes 262176 | tf_op jit(solution)/shard_map/ppermute | solution.py:362
  41.6 7.8 %collective-permute-done.9.refs_3_ = bf16[4,64,640]{2,1,0:T(8,128)(2,1)S(1)} collective-permute-done((bf16[4,64,640]{2,1,0:T(8,128)(2,1)S(1)}, bf16[4,64,640]{2,1,0:T(8,128)(2,1)S(1)}, u32[]{:S(2)}, u32[]{:S(2)}) %collective-permute-start.9) | collective-permute-done | bytes 327712 | tf_op jit(solution)/shard_map/ppermute | solution.py:362
  49.4 3.0 collective-permute-done.8.refs_1_
  53.4 2.0 collective-permute-start.14
  55.4 22.2 %collective-permute-done.14.refs_1_ = bf16[1,256,512]{2,1,0:T(8,128)(2,1)S(1)} collective-permute-done((bf16[1,256,512]{2,1,0:T(8,128)(2,1)S(1)}, bf16[1,256,512]{2,1,0:T(8,128)(2,1)S(1)}, u32[]{:S(2)}, u32[]{:S(2)}) %collective-permute-start.14) | collective-permute-done | bytes 262176 | tf_op jit(solution)/shard_map/ppermute | solution.py:362
  77.6 3.7 %collective-permute-done.13.refs_3_ = bf16[2,64,640]{2,1,0:T(8,128)(2,1)S(1)} collective-permute-done((bf16[2,64,640]{2,1,0:T(8,128)(2,1)S(1)}, bf16[2,64,640]{2,1,0:T(8,128)(2,1)S(1)}, u32[]{:S(2)}, u32[]{:S(2)}) %collective-permute-start.13) | collective-permute-done | bytes 163872 | tf_op jit(solution)/shard_map/ppermute | solution.py:362
  82.4 1.7 shard_map.275
  85.0 2.9 collective-permute-done.20.refs_7_
  89.1 9.7 %shard_map.277 = (bf16[1024,3072]{1,0:T(8,128)(2,1)}, bf16[1024,1024]{1,0:T(8,128)(2,1)S(1)}, bf16[1024,256]{1,0:T(8,128)(2,1)S(1)}, f32[448,3072]{1,0:T(8,128)}) custom-call(s32[1]{0:T(128)} %bitcast.16.me_ref, bf16[448,1024]{1,0:T(8,128)(2,1)S(1)} %pad_maximum_fusion.left_ref, bf16[8,64,1536]{2,1,0:T(8,128)(2,1)S(1)} %get-tuple-element.331.refs_0_, ...), custom_call_target="tpu_custom_call" | custom-call | flops 1 | bytes 1 | tf_op jit(solution)/shard_map/pallas_call | solution.py:517
  98.8 1.3 copy-done.8
  100.2 1.4 slice_reduce_fusion.1
  101.7 3.2 add_convert_fusion.query_ref.key_ref.value_ref
  105.0 2.9 shard_map.278
  107.9 1.4 collective-permute-start.25
  109.9 2.1 shard_map.279
  112.1 1.5 collective-permute-start.26
  113.9 8.5 %shard_map.280 = (bf16[256,1024]{1,0:T(8,128)(2,1)S(1)}, f32[8,2,256]{2,1,0:T(2,128)S(1)}) custom-call(s32[1,256]{1,0:T(1,128)S(1)} %bitcast.115, s32[448,1]{1,0:T(8,128)S(1)} %copy.37.key_docs, bf16[448,3072]{1,0:T(8,128)(2,1)S(1)} %add_convert_fusion.query_ref.key_ref.value_ref, bf16[448,3072]{1,0:T(8,128)(2,1)S(1)} %add_convert_fusion.query_ref.key_ref.value_ref, ...), custom_call_target="tpu_custom_call" | custom-call | flops 1 | bytes 1 | tf_op jit(solution)/shard_map/pallas_call | solution.py:800
  125.6 1.6 copy-done.9
  128.3 1.4 shard_map.281
  133.1 4.3 %collective-permute-done.24.refs_3_ = bf16[8,64,640]{2,1,0:T(8,128)(2,1)} collective-permute-done((bf16[8,64,640]{2,1,0:T(8,128)(2,1)}, bf16[8,64,640]{2,1,0:T(8,128)(2,1)}, u32[]{:S(2)}, u32[]{:S(2)}) %collective-permute-start.24) | collective-permute-done | bytes 655392 | tf_op jit(solution)/shard_map/ppermute | solution.py:362
  138.0 2.8 shard_map.282
  142.1 1.5 slice.176
  144.7 1.5 collective-permute-start.29
  147.3 7.1 %shard_map.283 = (bf16[1024,4096]{1,0:T(8,128)(2,1)}, f32[256,4096]{1,0:T(8,128)S(1)}) custom-call(s32[1]{0:T(128)} %bitcast.16.me_ref, bf16[256,1024]{1,0:T(8,128)(2,1)S(1)} %copy-done.15, bf16[8,64,1408]{2,1,0:T(8,128)(2,1)} %get-tuple-element.375.refs_0_, bf16[8,64,640]{2,1,0:T(8,128)(2,1)} %get-tuple-element.376.refs_1_, ...), custom_call_target="tpu_custom_call" | custom-call | flops 1 | bytes 1 | tf_op jit(solution)/shard_map/pallas_call | solution.py:517
  154.4 3.6 %fusion.4 = (f32[256,4096]{1,0:T(8,128)}, bf16[256,4096]{1,0:T(8,128)(2,1)}) fusion(f32[256,4096]{1,0:T(8,128)S(1)} %get-tuple-element.383, f32[4096]{0:T(1024)S(1)} %add.166), kind=kLoop, calls=%fused_computation.7 | loop fusion | flops 11534336 | bytes 10502144 | tf_op jit(solution)/shard_map/add | solution.py:1016
  158.8 2.4 collective-permute-done.28.refs_2_
  164.5 1.8 collective-permute-done.36.refs_7_
  166.3 1.6 copy-done
  168.9 6.7 %shard_map.284 = (bf16[4096,1024]{1,0:T(8,128)(2,1)}, f32[256,1024]{1,0:T(8,128)S(1)}) custom-call(s32[1]{0:T(128)} %bitcast.16.me_ref, bf16[256,4096]{1,0:T(8,128)(2,1)S(1)} %copy-done, bf16[8,256,384]{2,1,0:T(8,128)(2,1)} %get-tuple-element.385.refs_0_, bf16[8,256,128]{2,1,0:T(8,128)(2,1)S(1)} %get-tuple-element.386.refs_1_, ...), custom_call_target="tpu_custom_call" | custom-call | flops 1 | bytes 1 | tf_op jit(solution)/shard_map/pallas_call | solution.py:517
  177.0 1.6 fusion.24
  178.6 5.8 %shard_map.285 = (bf16[32,128,384]{2,1,0:T(8,128)(2,1)S(1)}, bf16[32,128,384]{2,1,0:T(8,128)(2,1)}, bf16[32,128,128]{2,1,0:T(8,128)(2,1)S(1)}, bf16[32,128,128]{2,1,0:T(8,128)(2,1)}) custom-call(s32[1]{0:T(128)} %bitcast.16.me_ref, bf16[256,4096]{1,0:T(8,128)(2,1)S(1)} %copy-done, bf16[256,1024]{1,0:T(8,128)(2,1)S(1)} %get-tuple-element.421.right_ref), custom_call_target="tpu_custom_call" | custom-call | flops 1 | bytes 1 | tf_op jit(solution)/shard_map/pallas_call | solution.py:598
  184.4 1.6 copy-done.1
  188.7 7.1 %convert_reduce_fusion = (bf16[4096]{0:T(1024)(128)(2,1)S(1)}, bf16[256,4096]{1,0:T(8,128)(2,1)S(1)}) fusion(f32[256,4096]{1,0:T(8,128)} %get-tuple-element.402, bf16[256,1024]{1,0:T(8,128)(2,1)S(1)} %get-tuple-element.421.right_ref, bf16[4096,1024]{1,0:T(8,128)(2,1)} %get-tuple-element.401), kind=kOutput, calls=%fused_computation.8 | convolution fusion | flops 2151673856 | bytes 15212544 | tf_op jit(solution)/shard_map/td,fd->tf/dot_general | solution.py:1036
  195.9 3.5 %shard_map.286 = (bf16[16,128,384]{2,1,0:T(8,128)(2,1)S(1)}, bf16[16,128,384]{2,1,0:T(8,128)(2,1)S(1)}, bf16[16,128,128]{2,1,0:T(8,128)(2,1)S(1)}, bf16[16,128,128]{2,1,0:T(8,128)(2,1)S(1)}) custom-call(bf16[32,128,384]{2,1,0:T(8,128)(2,1)S(1)} %copy-done.2, bf16[32,128,384]{2,1,0:T(8,128)(2,1)S(1)} %copy-done.2, ...), custom_call_target="tpu_custom_call" | custom-call | flops 1 | bytes 1 | tf_op jit(solution)/shard_map/pallas_call | solution.py:636
  199.4 1.5 collective-permute-start.40
  201.7 6.1 %multiply_reduce_fusion = (bf16[1024]{0:T(1024)(128)(2,1)S(1)}, f32[256]{0:T(256)S(1)}, f32[256]{0:T(256)S(1)}, bf16[1024]{0:T(1024)(128)(2,1)S(1)}, f32[256,1024]{1,0:T(8,128)S(1)}) fusion(f32[256,1024]{1,0:T(8,128)S(1)} %copy-done.20, f32[1024]{0:T(1024)S(1)} %mul.180, f32[256,1024]{1,0:T(8,128)S(1)} %copy-done.29, ...), kind=kOutput, calls=%fused_computation.26 | convolution fusion | flops 2149578240 | bytes 13641728 | tf_op jit(solution)/shard_map/tf,df->td/dot_general | solution.py:1051
  207.9 1.3 convert_reduce_fusion.3
  209.3 3.0 shard_map.287
  213.2 7.2 %collective-permute-done.39.refs_2_.refs_3_ = bf16[16,128,384]{2,1,0:T(8,128)(2,1)S(1)} collective-permute-done((bf16[16,128,384]{2,1,0:T(8,128)(2,1)S(1)}, bf16[16,128,384]{2,1,0:T(8,128)(2,1)S(1)}, u32[]{:S(2)}, u32[]{:S(2)}) %collective-permute-start.39) | collective-permute-done | bytes 1572896 | tf_op jit(solution)/shard_map/ppermute | solution.py:362
  220.4 1.5 collective-permute-start.43
  222.8 9.6 %shard_map.289 = (bf16[448,3072]{1,0:T(8,128)(2,1)S(1)}, f32[2,1,1024]{2,1,0:T(1,128)S(1)}) custom-call(s32[1,256]{1,0:T(1,128)S(1)} %bitcast.116, s32[448,1]{1,0:T(8,128)S(1)} %copy.37.key_docs, bf16[448,3072]{1,0:T(8,128)(2,1)S(1)} %add_convert_fusion.query_ref.key_ref.value_ref, bf16[448,3072]{1,0:T(8,128)(2,1)S(1)} %add_convert_fusion.query_ref.key_ref.value_ref, ...), custom_call_target="tpu_custom_call" | custom-call | flops 1 | bytes 1 | tf_op jit(solution)/shard_map/pallas_call | solution.py:866
  236.1 1.5 collective-permute-start.48
  238.3 3.8 %shard_map.292 = (bf16[32,32,1536]{2,1,0:T(8,128)(2,1)S(1)}, bf16[32,32,1536]{2,1,0:T(8,128)(2,1)S(1)}) custom-call(s32[1]{0:T(128)} %bitcast.16.me_ref, bf16[448,1024]{1,0:T(8,128)(2,1)S(1)} %copy-done.4, bf16[448,3072]{1,0:T(8,128)(2,1)S(1)} %get-tuple-element.456.right_ref.grad_ref), custom_call_target="tpu_custom_call" | custom-call | flops 1 | bytes 1 | tf_op jit(solution)/shard_map/pallas_call | solution.py:598
  243.2 8.9 %collective-permute-done.48.refs_6_.refs_7_ = bf16[16,32,640]{2,1,0:T(8,128)(2,1)S(1)} collective-permute-done((bf16[16,32,640]{2,1,0:T(8,128)(2,1)S(1)}, bf16[16,32,640]{2,1,0:T(8,128)(2,1)S(1)}, u32[]{:S(2)}, u32[]{:S(2)}) %collective-permute-start.48) | collective-permute-done | bytes 655392 | tf_op jit(solution)/shard_map/ppermute | solution.py:362
  252.1 3.6 %collective-permute-done.47.refs_2_.refs_3_ = bf16[16,32,1408]{2,1,0:T(8,128)(2,1)S(1)} collective-permute-done((bf16[16,32,1408]{2,1,0:T(8,128)(2,1)S(1)}, bf16[16,32,1408]{2,1,0:T(8,128)(2,1)S(1)}, u32[]{:S(2)}, u32[]{:S(2)}) %collective-permute-start.47) | collective-permute-done | bytes 1441824 | tf_op jit(solution)/shard_map/ppermute | solution.py:362
  255.7 3.0 collective-permute-start.52
  260.0 1.4 collective-permute-start.49
  261.5 3.7 %shard_map.296 = (f32[256,1024]{1,0:T(8,128)S(1)}, bf16[192,1024]{1,0:T(8,128)(2,1)S(1)}) custom-call(bf16[448,3072]{1,0:T(8,128)(2,1)S(1)} %get-tuple-element.456.right_ref.grad_ref, bf16[1024,3072]{1,0:T(8,128)(2,1)S(1)} %bitcast.110), custom_call_target="tpu_custom_call" | custom-call | flops 1 | bytes 1 | tf_op jit(solution)/shard_map/pallas_call | solution.py:693
  265.3 5.5 %collective-permute-done.49 = bf16[2,128,512]{2,1,0:T(8,128)(2,1)S(1)} collective-permute-done((bf16[2,128,512]{2,1,0:T(8,128)(2,1)S(1)}, bf16[2,128,512]{2,1,0:T(8,128)(2,1)S(1)}, u32[]{:S(2)}, u32[]{:S(2)}) %collective-permute-start.49) | collective-permute-done | bytes 262176 | tf_op jit(solution)/shard_map/ppermute | solution.py:362
  271.9 2.1 collective-permute-start.58
  274.3 1.5 collective-permute-start.56
  277.1 7.1 %collective-permute-start.54 = (bf16[128,512]{1,0:T(8,128)(2,1)S(1)}, bf16[128,512]{1,0:T(8,128)(2,1)S(1)}, u32[]{:S(2)}, u32[]{:S(2)}) collective-permute-start(bf16[128,512]{1,0:T(8,128)(2,1)S(1)} %get-tuple-element.587), channel_id=1, source_target_pairs={{0,1},{1,0},{2,3},{3,2},{4,5},{5,4},{6,7},{7,6},{8,9},{9,8},{10,11... | collective-permute-start | bytes 393224 | tf_op jit(solution)/shard_map/ppermute | solution.py:362
  285.2 11.5 %collective-permute-done.56.refs_6_.refs_7_ = bf16[4,32,640]{2,1,0:T(8,128)(2,1)S(1)} collective-permute-done((bf16[4,32,640]{2,1,0:T(8,128)(2,1)S(1)}, bf16[4,32,640]{2,1,0:T(8,128)(2,1)S(1)}, u32[]{:S(2)}, u32[]{:S(2)}) %collective-permute-start.56) | collective-permute-done | bytes 163872 | tf_op jit(solution)/shard_map/ppermute | solution.py:362
  300.5 7.1 %collective-permute-done.59 = bf16[2,32,2048]{2,1,0:T(8,128)(2,1)S(1)} collective-permute-done((bf16[2,32,2048]{2,1,0:T(8,128)(2,1)S(1)}, bf16[2,32,2048]{2,1,0:T(8,128)(2,1)S(1)}, u32[]{:S(2)}, u32[]{:S(2)}) %collective-permute-start.59) | collective-permute-done | bytes 262176 | tf_op jit(solution)/shard_map/ppermute | solution.py:362
  310.9 10.4 %collective-permute-start.62 = (bf16[32,2048]{1,0:T(8,128)(2,1)}, bf16[32,2048]{1,0:T(8,128)(2,1)S(1)}, u32[]{:S(2)}, u32[]{:S(2)}) collective-permute-start(bf16[32,2048]{1,0:T(8,128)(2,1)} %get-tuple-element.585), channel_id=1, source_target_pairs={{0,1},{1,0},{2,3},{3,2},{4,5},{5,4},{6,7},{7,6},{8,9},{9,8},{10,11... | collective-permute-start | bytes 393224 | tf_op jit(solution)/shard_map/ppermute | solution.py:362
  322.7 1.7 collective-permute-start.65
  324.4 1.7 collective-permute-start.66
  327.0 5.0 %collective-permute-done.65 = bf16[2,32,2176]{2,1,0:T(8,128)(2,1)S(1)} collective-permute-done((bf16[2,32,2176]{2,1,0:T(8,128)(2,1)S(1)}, bf16[2,32,2176]{2,1,0:T(8,128)(2,1)S(1)}, u32[]{:S(2)}, u32[]{:S(2)}) %collective-permute-start.65) | collective-permute-done | bytes 278560 | tf_op jit(solution)/shard_map/ppermute | solution.py:362
  332.1 8.0 %collective-permute-start.67 = (bf16[32,2176]{1,0:T(8,128)(2,1)S(1)}, bf16[32,2176]{1,0:T(8,128)(2,1)S(1)}, u32[]{:S(2)}, u32[]{:S(2)}) collective-permute-start(bf16[32,2176]{1,0:T(8,128)(2,1)S(1)} %fusion.19), channel_id=1, source_target_pairs={{0,1},{1,0},{2,3},{3,2},{4,5},{5,4},{6,7},{7,6},{8,9},{9,8},{10,11... | collective-permute-start | bytes 417800 | tf_op jit(solution)/shard_map/ppermute | solution.py:362
  (272 shorter events, 61.6 us)
Async XLA Ops:
  5.2 5.8 %collective-permute-start.3 = (bf16[128,512]{1,0:T(8,128)(2,1)S(1)}, bf16[128,512]{1,0:T(8,128)(2,1)S(1)}, u32[]{:S(2)}, u32[]{:S(2)}) collective-permute-start(bf16[128,512]{1,0:T(8,128)(2,1)S(1)} %get-tuple-element.599), channel_id=1, source_target_pairs={{0,1},{1,0},{2,3},{3,2},{4,5},{5,4},{6,7},{7,6},{8,9},{9,8},{10,11... | collective-permute-start | bytes 393224 | tf_op jit(solution)/shard_map/ppermute | solution.py:362
  6.9 16.8 %collective-permute-start.1 = (bf16[1,64,2176]{2,1,0:T(8,128)(2,1)S(1)}, bf16[1,64,2176]{2,1,0:T(8,128)(2,1)S(1)}, u32[]{:S(2)}, u32[]{:S(2)}) collective-permute-start(bf16[1,64,2176]{2,1,0:T(8,128)(2,1)S(1)} %maximum_bitcast_fusion.refs_0_), channel_id=1, source_target_pairs={{0,8},{1,9},{2,10},{3,11},{4,12},{5,13},{6,14},{7,15},{8,0},{9,1},... | collective-permute-start | bytes 835592 | tf_op jit(solution)/shard_map/ppermute | solution.py:362
  23.7 16.7 %collective-permute-start.7 = (bf16[192,1024]{1,0:T(8,128)(2,1)S(1)}, bf16[192,1024]{1,0:T(8,128)(2,1)S(1)}, u32[]{:S(2)}, u32[]{:S(2)}) collective-permute-start(bf16[192,1024]{1,0:T(8,128)(2,1)S(1)} %constant_dynamic-slice_fusion.1), channel_id=1, source_target_pairs={{0,16},{16,0},{1,17},{17,1},{2,18},{18,2},{3,19},{19,3},{4,20},{20... | collective-permute-start | bytes 1179656 | tf_op jit(solution)/shard_map/ppermute | solution.py:958
  24.9 15.5 %collective-permute-start.4 = (bf16[2,64,1536]{2,1,0:T(8,128)(2,1)S(1)}, bf16[2,64,1536]{2,1,0:T(8,128)(2,1)S(1)}, u32[]{:S(2)}, u32[]{:S(2)}) collective-permute-start(bf16[2,64,1536]{2,1,0:T(8,128)(2,1)S(1)} %get-tuple-element.295.refs_0_), channel_id=1, source_target_pairs={{0,16},{1,3},{2,18},{3,1},{4,20},{5,7},{6,22},{7,5},{8,24},{9,11},... | collective-permute-start | bytes 1179656 | tf_op jit(solution)/shard_map/ppermute | solution.py:362
  26.3 14.1 %collective-permute-start.6 = (bf16[1,64,2048]{2,1,0:T(8,128)(2,1)S(1)}, bf16[1,64,2048]{2,1,0:T(8,128)(2,1)S(1)}, u32[]{:S(2)}, u32[]{:S(2)}) collective-permute-start(bf16[1,64,2048]{2,1,0:T(8,128)(2,1)S(1)} %maximum_bitcast_fusion.1.refs_0_), channel_id=1, source_target_pairs={{0,8},{1,9},{2,10},{3,11},{4,12},{5,13},{6,14},{7,15},{8,0},{9,1},... | collective-permute-start | bytes 786440 | tf_op jit(solution)/shard_map/ppermute | solution.py:362
  26.4 9.2 %collective-permute-start.5 = (bf16[2,64,640]{2,1,0:T(8,128)(2,1)S(1)}, bf16[2,64,640]{2,1,0:T(8,128)(2,1)S(1)}, u32[]{:S(2)}, u32[]{:S(2)}) collective-permute-start(bf16[2,64,640]{2,1,0:T(8,128)(2,1)S(1)} %get-tuple-element.297.refs_2_), channel_id=1, source_target_pairs={{0,4},{1,5},{2,6},{3,7},{4,0},{5,1},{6,2},{7,3},{8,12},{9,13},{10,... | collective-permute-start | bytes 491528 | tf_op jit(solution)/shard_map/ppermute | solution.py:362
  41.2 11.2 %collective-permute-start.8 = (bf16[4,64,1536]{2,1,0:T(8,128)(2,1)S(1)}, bf16[4,64,1536]{2,1,0:T(8,128)(2,1)S(1)}, u32[]{:S(2)}, u32[]{:S(2)}) collective-permute-start(bf16[4,64,1536]{2,1,0:T(8,128)(2,1)S(1)} %get-tuple-element.304.refs_0_), channel_id=1, source_target_pairs={{0,4},{1,17},{2,6},{3,19},{4,0},{5,21},{6,2},{7,23},{8,12},{9,25},... | collective-permute-start | bytes 2359304 | tf_op jit(solution)/shard_map/ppermute | solution.py:362
  41.3 8.1 %collective-permute-start.9 = (bf16[4,64,640]{2,1,0:T(8,128)(2,1)S(1)}, bf16[4,64,640]{2,1,0:T(8,128)(2,1)S(1)}, u32[]{:S(2)}, u32[]{:S(2)}) collective-permute-start(bf16[4,64,640]{2,1,0:T(8,128)(2,1)S(1)} %get-tuple-element.306.refs_2_), channel_id=1, source_target_pairs={{0,2},{1,3},{2,0},{3,1},{4,6},{5,7},{6,4},{7,5},{8,10},{9,11},{10,... | collective-permute-start | bytes 983048 | tf_op jit(solution)/shard_map/ppermute | solution.py:362
  52.8 28.5 %collective-permute-start.10 = (bf16[8,64,1536]{2,1,0:T(8,128)(2,1)S(1)}, bf16[8,64,1536]{2,1,0:T(8,128)(2,1)S(1)}, u32[]{:S(2)}, u32[]{:S(2)}) collective-permute-start(bf16[8,64,1536]{2,1,0:T(8,128)(2,1)S(1)} %get-tuple-element.331.refs_0_), channel_id=1, source_target_pairs={{0,2},{1,5},{2,0},{3,7},{4,6},{5,1},{6,4},{7,3},{8,10},{9,13},{10,... | collective-permute-start | bytes 4718600 | tf_op jit(solution)/shard_map/ppermute | solution.py:362
  52.9 28.4 %collective-permute-start.11 = (bf16[8,64,640]{2,1,0:T(8,128)(2,1)S(1)}, bf16[8,64,640]{2,1,0:T(8,128)(2,1)S(1)}, u32[]{:S(2)}, u32[]{:S(2)}) collective-permute-start(bf16[8,64,640]{2,1,0:T(8,128)(2,1)S(1)} %get-tuple-element.332.refs_1_), channel_id=1, source_target_pairs={{0,16},{1,17},{2,18},{3,19},{4,20},{5,21},{6,22},{7,23},{8,24},{9,... | collective-permute-start | bytes 1966088 | tf_op jit(solution)/shard_map/ppermute | solution.py:362
  53.1 28.1 %collective-permute-start.12 = (bf16[2,64,1408]{2,1,0:T(8,128)(2,1)S(1)}, bf16[2,64,1408]{2,1,0:T(8,128)(2,1)S(1)}, u32[]{:S(2)}, u32[]{:S(2)}) collective-permute-start(bf16[2,64,1408]{2,1,0:T(8,128)(2,1)S(1)} %get-tuple-element.316.refs_0_), channel_id=1, source_target_pairs={{0,16},{1,3},{2,18},{3,1},{4,20},{5,7},{6,22},{7,5},{8,24},{9,11},... | collective-permute-start | bytes 1081352 | tf_op jit(solution)/shard_map/ppermute | solution.py:362
  53.4 24.2 %collective-permute-start.14 = (bf16[1,256,512]{2,1,0:T(8,128)(2,1)S(1)}, bf16[1,256,512]{2,1,0:T(8,128)(2,1)S(1)}, u32[]{:S(2)}, u32[]{:S(2)}) collective-permute-start(bf16[1,256,512]{2,1,0:T(8,128)(2,1)S(1)} %maximum_bitcast_fusion.2.refs_0_), channel_id=1, source_target_pairs={{0,8},{1,9},{2,10},{3,11},{4,12},{5,13},{6,14},{7,15},{8,0},{9,1},... | collective-permute-start | bytes 786440 | tf_op jit(solution)/shard_map/ppermute | solution.py:362
  55.3 25.9 %collective-permute-start.13 = (bf16[2,64,640]{2,1,0:T(8,128)(2,1)S(1)}, bf16[2,64,640]{2,1,0:T(8,128)(2,1)S(1)}, u32[]{:S(2)}, u32[]{:S(2)}) collective-permute-start(bf16[2,64,640]{2,1,0:T(8,128)(2,1)S(1)} %get-tuple-element.318.refs_2_), channel_id=1, source_target_pairs={{0,4},{1,5},{2,6},{3,7},{4,0},{5,1},{6,2},{7,3},{8,12},{9,13},{10,... | collective-permute-start | bytes 491528 | tf_op jit(solution)/shard_map/ppermute | solution.py:362
  81.3 7.6 %collective-permute-start.19 = (bf16[8,64,1536]{2,1,0:T(8,128)(2,1)S(1)}, bf16[8,64,1536]{2,1,0:T(8,128)(2,1)S(1)}, u32[]{:S(2)}, u32[]{:S(2)}) collective-permute-start(bf16[8,64,1536]{2,1,0:T(8,128)(2,1)S(1)} %collective-permute-done.10.refs_2_), channel_id=1, source_target_pairs={{0,1},{1,0},{2,3},{3,2},{4,5},{5,4},{6,7},{7,6},{8,9},{9,8},{10,11... | collective-permute-start | bytes 4718600 | tf_op jit(solution)/shard_map/ppermute | solution.py:362
  81.4 7.7 %collective-permute-start.21 = (bf16[8,64,1536]{2,1,0:T(8,128)(2,1)S(1)}, bf16[8,64,1536]{2,1,0:T(8,128)(2,1)S(1)}, u32[]{:S(2)}, u32[]{:S(2)}) collective-permute-start(bf16[8,64,1536]{2,1,0:T(8,128)(2,1)S(1)} %get-tuple-element.331.refs_0_), channel_id=1, source_target_pairs={{0,1},{1,0},{2,3},{3,2},{4,5},{5,4},{6,7},{7,6},{8,9},{9,8},{10,11... | collective-permute-start | bytes 4718600 | tf_op jit(solution)/shard_map/ppermute | solution.py:362
  81.9 6.1 %collective-permute-start.20 = (bf16[8,64,640]{2,1,0:T(8,128)(2,1)S(1)}, bf16[8,64,640]{2,1,0:T(8,128)(2,1)S(1)}, u32[]{:S(2)}, u32[]{:S(2)}) collective-permute-start(bf16[8,64,640]{2,1,0:T(8,128)(2,1)S(1)} %collective-permute-done.11.refs_3_), channel_id=1, source_target_pairs={{0,1},{1,0},{2,3},{3,2},{4,5},{5,4},{6,7},{7,6},{8,9},{9,8},{10,11... | collective-permute-start | bytes 1966088 | tf_op jit(solution)/shard_map/ppermute | solution.py:362
  81.9 6.9 %collective-permute-start.22 = (bf16[8,64,640]{2,1,0:T(8,128)(2,1)S(1)}, bf16[8,64,640]{2,1,0:T(8,128)(2,1)S(1)}, u32[]{:S(2)}, u32[]{:S(2)}) collective-permute-start(bf16[8,64,640]{2,1,0:T(8,128)(2,1)S(1)} %get-tuple-element.332.refs_1_), channel_id=1, source_target_pairs={{0,1},{1,0},{2,3},{3,2},{4,5},{5,4},{6,7},{7,6},{8,9},{9,8},{10,11... | collective-permute-start | bytes 1966088 | tf_op jit(solution)/shard_map/ppermute | solution.py:362
  84.1 20.8 %collective-permute-start.16 = (bf16[4,64,640]{2,1,0:T(8,128)(2,1)}, bf16[4,64,640]{2,1,0:T(8,128)(2,1)}, u32[]{:S(2)}, u32[]{:S(2)}) collective-permute-start(bf16[4,64,640]{2,1,0:T(8,128)(2,1)} %get-tuple-element.343.refs_2_), channel_id=1, source_target_pairs={{0,2},{1,3},{2,0},{3,1},{4,6},{5,7},{6,4},{7,5},{8,10},{9,11},{10,... | collective-permute-start | bytes 983048 | tf_op jit(solution)/shard_map/ppermute | solution.py:362
  87.9 17.0 %collective-permute-start.18 = (bf16[2,256,128]{2,1,0:T(8,128)(2,1)S(1)}, bf16[2,256,128]{2,1,0:T(8,128)(2,1)S(1)}, u32[]{:S(2)}, u32[]{:S(2)}) collective-permute-start(bf16[2,256,128]{2,1,0:T(8,128)(2,1)S(1)} %get-tuple-element.349.refs_2_), channel_id=1, source_target_pairs={{0,4},{1,5},{2,6},{3,7},{4,0},{5,1},{6,2},{7,3},{8,12},{9,13},{10,... | collective-permute-start | bytes 393224 | tf_op jit(solution)/shard_map/ppermute | solution.py:362
  88.9 16.1 %collective-permute-start.17 = (bf16[2,256,384]{2,1,0:T(8,128)(2,1)}, bf16[2,256,384]{2,1,0:T(8,128)(2,1)}, u32[]{:S(2)}, u32[]{:S(2)}) collective-permute-start(bf16[2,256,384]{2,1,0:T(8,128)(2,1)} %get-tuple-element.347.refs_0_), channel_id=1, source_target_pairs={{0,16},{1,3},{2,18},{3,1},{4,20},{5,7},{6,22},{7,5},{8,24},{9,11},... | collective-permute-start | bytes 1179656 | tf_op jit(solution)/shard_map/ppermute | solution.py:362
  88.9 16.1 %collective-permute-start.15 = (bf16[4,64,1408]{2,1,0:T(8,128)(2,1)}, bf16[4,64,1408]{2,1,0:T(8,128)(2,1)}, u32[]{:S(2)}, u32[]{:S(2)}) collective-permute-start(bf16[4,64,1408]{2,1,0:T(8,128)(2,1)} %get-tuple-element.341.refs_0_), channel_id=1, source_target_pairs={{0,4},{1,17},{2,6},{3,19},{4,0},{5,21},{6,2},{7,23},{8,12},{9,25},... | collective-permute-start | bytes 2162696 | tf_op jit(solution)/shard_map/ppermute | solution.py:362
  107.9 29.5 %collective-permute-start.25 = (bf16[8,64,1408]{2,1,0:T(8,128)(2,1)}, bf16[8,64,1408]{2,1,0:T(8,128)(2,1)}, u32[]{:S(2)}, u32[]{:S(2)}) collective-permute-start(bf16[8,64,1408]{2,1,0:T(8,128)(2,1)} %get-tuple-element.375.refs_0_), channel_id=1, source_target_pairs={{0,1},{1,0},{2,3},{3,2},{4,5},{5,4},{6,7},{7,6},{8,9},{9,8},{10,11... | collective-permute-start | bytes 4325384 | tf_op jit(solution)/shard_map/ppermute | solution.py:362
  109.3 28.1 %collective-permute-start.23 = (bf16[8,64,1408]{2,1,0:T(8,128)(2,1)}, bf16[8,64,1408]{2,1,0:T(8,128)(2,1)}, u32[]{:S(2)}, u32[]{:S(2)}) collective-permute-start(bf16[8,64,1408]{2,1,0:T(8,128)(2,1)} %get-tuple-element.375.refs_0_), channel_id=1, source_target_pairs={{0,2},{1,5},{2,0},{3,7},{4,6},{5,1},{6,4},{7,3},{8,10},{9,13},{10,... | collective-permute-start | bytes 4325384 | tf_op jit(solution)/shard_map/ppermute | solution.py:362
  112.1 25.3 %collective-permute-start.26 = (bf16[4,256,384]{2,1,0:T(8,128)(2,1)}, bf16[4,256,384]{2,1,0:T(8,128)(2,1)}, u32[]{:S(2)}, u32[]{:S(2)}) collective-permute-start(bf16[4,256,384]{2,1,0:T(8,128)(2,1)} %get-tuple-element.363.refs_0_), channel_id=1, source_target_pairs={{0,4},{1,17},{2,6},{3,19},{4,0},{5,21},{6,2},{7,23},{8,12},{9,25},... | collective-permute-start | bytes 2359304 | tf_op jit(solution)/shard_map/ppermute | solution.py:362
  113.6 23.7 %collective-permute-start.24 = (bf16[8,64,640]{2,1,0:T(8,128)(2,1)}, bf16[8,64,640]{2,1,0:T(8,128)(2,1)}, u32[]{:S(2)}, u32[]{:S(2)}) collective-permute-start(bf16[8,64,640]{2,1,0:T(8,128)(2,1)} %get-tuple-element.376.refs_1_), channel_id=1, source_target_pairs={{0,16},{1,17},{2,18},{3,19},{4,20},{5,21},{6,22},{7,23},{8,24},{9,... | collective-permute-start | bytes 1966088 | tf_op jit(solution)/shard_map/ppermute | solution.py:362
  113.7 19.4 %collective-permute-start.27 = (bf16[4,256,128]{2,1,0:T(8,128)(2,1)}, bf16[4,256,128]{2,1,0:T(8,128)(2,1)}, u32[]{:S(2)}, u32[]{:S(2)}) collective-permute-start(bf16[4,256,128]{2,1,0:T(8,128)(2,1)} %get-tuple-element.365.refs_2_), channel_id=1, source_target_pairs={{0,2},{1,3},{2,0},{3,1},{4,6},{5,7},{6,4},{7,5},{8,10},{9,11},{10,... | collective-permute-start | bytes 786440 | tf_op jit(solution)/shard_map/ppermute | solution.py:362
  137.4 8.8 %collective-permute-start.32 = (bf16[8,64,1408]{2,1,0:T(8,128)(2,1)}, bf16[8,64,1408]{2,1,0:T(8,128)(2,1)}, u32[]{:S(2)}, u32[]{:S(2)}) collective-permute-start(bf16[8,64,1408]{2,1,0:T(8,128)(2,1)} %collective-permute-done.23.refs_2_), channel_id=1, source_target_pairs={{0,1},{1,0},{2,3},{3,2},{4,5},{5,4},{6,7},{7,6},{8,9},{9,8},{10,11... | collective-permute-start | bytes 4325384 | tf_op jit(solution)/shard_map/ppermute | solution.py:362
  137.5 7.1 %collective-permute-start.33 = (bf16[8,64,640]{2,1,0:T(8,128)(2,1)}, bf16[8,64,640]{2,1,0:T(8,128)(2,1)}, u32[]{:S(2)}, u32[]{:S(2)}) collective-permute-start(bf16[8,64,640]{2,1,0:T(8,128)(2,1)} %collective-permute-done.24.refs_3_), channel_id=1, source_target_pairs={{0,1},{1,0},{2,3},{3,2},{4,5},{5,4},{6,7},{7,6},{8,9},{9,8},{10,11... | collective-permute-start | bytes 1966088 | tf_op jit(solution)/shard_map/ppermute | solution.py:362
  138.0 6.7 %collective-permute-start.34 = (bf16[8,64,640]{2,1,0:T(8,128)(2,1)}, bf16[8,64,640]{2,1,0:T(8,128)(2,1)}, u32[]{:S(2)}, u32[]{:S(2)}) collective-permute-start(bf16[8,64,640]{2,1,0:T(8,128)(2,1)} %get-tuple-element.376.refs_1_), channel_id=1, source_target_pairs={{0,1},{1,0},{2,3},{3,2},{4,5},{5,4},{6,7},{7,6},{8,9},{9,8},{10,11... | collective-permute-start | bytes 1966088 | tf_op jit(solution)/shard_map/ppermute | solution.py:362
  140.8 18.0 %collective-permute-start.30 = (bf16[8,256,384]{2,1,0:T(8,128)(2,1)}, bf16[8,256,384]{2,1,0:T(8,128)(2,1)}, u32[]{:S(2)}, u32[]{:S(2)}) collective-permute-start(bf16[8,256,384]{2,1,0:T(8,128)(2,1)} %get-tuple-element.385.refs_0_), channel_id=1, source_target_pairs={{0,1},{1,0},{2,3},{3,2},{4,5},{5,4},{6,7},{7,6},{8,9},{9,8},{10,11... | collective-permute-start | bytes 4718600 | tf_op jit(solution)/shard_map/ppermute | solution.py:362
  141.3 19.9 %collective-permute-start.28 = (bf16[8,256,384]{2,1,0:T(8,128)(2,1)}, bf16[8,256,384]{2,1,0:T(8,128)(2,1)}, u32[]{:S(2)}, u32[]{:S(2)}) collective-permute-start(bf16[8,256,384]{2,1,0:T(8,128)(2,1)} %get-tuple-element.385.refs_0_), channel_id=1, source_target_pairs={{0,2},{1,5},{2,0},{3,7},{4,6},{5,1},{6,4},{7,3},{8,10},{9,13},{10,... | collective-permute-start | bytes 4718600 | tf_op jit(solution)/shard_map/ppermute | solution.py:362
  144.6 13.4 %collective-permute-start.31 = (bf16[8,256,128]{2,1,0:T(8,128)(2,1)S(1)}, bf16[8,256,128]{2,1,0:T(8,128)(2,1)S(1)}, u32[]{:S(2)}, u32[]{:S(2)}) collective-permute-start(bf16[8,256,128]{2,1,0:T(8,128)(2,1)S(1)} %get-tuple-element.386.refs_1_), channel_id=1, source_target_pairs={{0,1},{1,0},{2,3},{3,2},{4,5},{5,4},{6,7},{7,6},{8,9},{9,8},{10,11... | collective-permute-start | bytes 1572872 | tf_op jit(solution)/shard_map/ppermute | solution.py:362
  144.7 14.1 %collective-permute-start.29 = (bf16[8,256,128]{2,1,0:T(8,128)(2,1)S(1)}, bf16[8,256,128]{2,1,0:T(8,128)(2,1)}, u32[]{:S(2)}, u32[]{:S(2)}) collective-permute-start(bf16[8,256,128]{2,1,0:T(8,128)(2,1)S(1)} %get-tuple-element.386.refs_1_), channel_id=1, source_target_pairs={{0,16},{1,17},{2,18},{3,19},{4,20},{5,21},{6,22},{7,23},{8,24},{9,... | collective-permute-start | bytes 1572872 | tf_op jit(solution)/shard_map/ppermute | solution.py:362
  187.0 8.9 %collective-permute-start.37 = (bf16[32,128,384]{2,1,0:T(8,128)(2,1)}, bf16[32,128,384]{2,1,0:T(8,128)(2,1)}, u32[]{:S(2)}, u32[]{:S(2)}) collective-permute-start(bf16[32,128,384]{2,1,0:T(8,128)(2,1)} %get-tuple-element.396), channel_id=1, source_target_pairs={{0,1},{1,0},{2,3},{3,2},{4,5},{5,4},{6,7},{7,6},{8,9},{9,8},{10,11... | collective-permute-start | bytes 9437192 | tf_op jit(solution)/shard_map/ppermute | solution.py:362
  187.4 8.5 %collective-permute-start.38 = (bf16[32,128,128]{2,1,0:T(8,128)(2,1)}, bf16[32,128,128]{2,1,0:T(8,128)(2,1)}, u32[]{:S(2)}, u32[]{:S(2)}) collective-permute-start(bf16[32,128,128]{2,1,0:T(8,128)(2,1)} %get-tuple-element.397), channel_id=1, source_target_pairs={{0,1},{1,0},{2,3},{3,2},{4,5},{5,4},{6,7},{7,6},{8,9},{9,8},{10,11... | collective-permute-start | bytes 3145736 | tf_op jit(solution)/shard_map/ppermute | solution.py:362
  199.4 13.9 %collective-permute-start.40 = (bf16[16,128,128]{2,1,0:T(8,128)(2,1)S(1)}, bf16[16,128,128]{2,1,0:T(8,128)(2,1)S(1)}, u32[]{:S(2)}, u32[]{:S(2)}) collective-permute-start(bf16[16,128,128]{2,1,0:T(8,128)(2,1)S(1)} %get-tuple-element.409), channel_id=1, source_target_pairs={{0,16},{1,17},{2,18},{3,19},{4,20},{5,21},{6,22},{7,23},{8,24},{9,... | collective-permute-start | bytes 1572872 | tf_op jit(solution)/shard_map/ppermute | solution.py:362
  200.9 19.6 %collective-permute-start.39 = (bf16[16,128,384]{2,1,0:T(8,128)(2,1)S(1)}, bf16[16,128,384]{2,1,0:T(8,128)(2,1)S(1)}, u32[]{:S(2)}, u32[]{:S(2)}) collective-permute-start(bf16[16,128,384]{2,1,0:T(8,128)(2,1)S(1)} %get-tuple-element.408), channel_id=1, source_target_pairs={{0,2},{1,5},{2,0},{3,7},{4,6},{5,1},{6,4},{7,3},{8,10},{9,13},{10,... | collective-permute-start | bytes 4718600 | tf_op jit(solution)/shard_map/ppermute | solution.py:362
  220.4 13.3 %collective-permute-start.43 = (bf16[32,32,1408]{2,1,0:T(8,128)(2,1)S(1)}, bf16[32,32,1408]{2,1,0:T(8,128)(2,1)S(1)}, u32[]{:S(2)}, u32[]{:S(2)}) collective-permute-start(bf16[32,32,1408]{2,1,0:T(8,128)(2,1)S(1)} %get-tuple-element.432), channel_id=1, source_target_pairs={{0,1},{1,0},{2,3},{3,2},{4,5},{5,4},{6,7},{7,6},{8,9},{9,8},{10,11... | collective-permute-start | bytes 8650760 | tf_op jit(solution)/shard_map/ppermute | solution.py:362
  221.9 11.8 %collective-permute-start.44 = (bf16[32,32,640]{2,1,0:T(8,128)(2,1)S(1)}, bf16[32,32,640]{2,1,0:T(8,128)(2,1)S(1)}, u32[]{:S(2)}, u32[]{:S(2)}) collective-permute-start(bf16[32,32,640]{2,1,0:T(8,128)(2,1)S(1)} %get-tuple-element.433), channel_id=1, source_target_pairs={{0,1},{1,0},{2,3},{3,2},{4,5},{5,4},{6,7},{7,6},{8,9},{9,8},{10,11... | collective-permute-start | bytes 3932168 | tf_op jit(solution)/shard_map/ppermute | solution.py:362
  222.5 11.2 %collective-permute-start.41 = (bf16[8,128,384]{2,1,0:T(8,128)(2,1)S(1)}, bf16[8,128,384]{2,1,0:T(8,128)(2,1)S(1)}, u32[]{:S(2)}, u32[]{:S(2)}) collective-permute-start(bf16[8,128,384]{2,1,0:T(8,128)(2,1)S(1)} %get-tuple-element.428), channel_id=1, source_target_pairs={{0,4},{1,17},{2,6},{3,19},{4,0},{5,21},{6,2},{7,23},{8,12},{9,25},... | collective-permute-start | bytes 2359304 | tf_op jit(solution)/shard_map/ppermute | solution.py:362
  222.6 9.8 %collective-permute-start.42 = (bf16[8,128,128]{2,1,0:T(8,128)(2,1)S(1)}, bf16[8,128,128]{2,1,0:T(8,128)(2,1)S(1)}, u32[]{:S(2)}, u32[]{:S(2)}) collective-permute-start(bf16[8,128,128]{2,1,0:T(8,128)(2,1)S(1)} %get-tuple-element.429), channel_id=1, source_target_pairs={{0,2},{1,3},{2,0},{3,1},{4,6},{5,7},{6,4},{7,5},{8,10},{9,11},{10,... | collective-permute-start | bytes 786440 | tf_op jit(solution)/shard_map/ppermute | solution.py:362
  234.1 9.1 %collective-permute-start.46 = (bf16[4,128,128]{2,1,0:T(8,128)(2,1)S(1)}, bf16[4,128,128]{2,1,0:T(8,128)(2,1)S(1)}, u32[]{:S(2)}, u32[]{:S(2)}) collective-permute-start(bf16[4,128,128]{2,1,0:T(8,128)(2,1)S(1)} %get-tuple-element.445), channel_id=1, source_target_pairs={{0,4},{1,5},{2,6},{3,7},{4,0},{5,1},{6,2},{7,3},{8,12},{9,13},{10,... | collective-permute-start | bytes 393224 | tf_op jit(solution)/shard_map/ppermute | solution.py:362
  234.9 8.2 %collective-permute-start.45 = (bf16[4,128,384]{2,1,0:T(8,128)(2,1)S(1)}, bf16[4,128,384]{2,1,0:T(8,128)(2,1)S(1)}, u32[]{:S(2)}, u32[]{:S(2)}) collective-permute-start(bf16[4,128,384]{2,1,0:T(8,128)(2,1)S(1)} %get-tuple-element.444), channel_id=1, source_target_pairs={{0,16},{1,3},{2,18},{3,1},{4,20},{5,7},{6,22},{7,5},{8,24},{9,11},... | collective-permute-start | bytes 1179656 | tf_op jit(solution)/shard_map/ppermute | solution.py:362
  236.1 16.0 %collective-permute-start.48 = (bf16[16,32,640]{2,1,0:T(8,128)(2,1)S(1)}, bf16[16,32,640]{2,1,0:T(8,128)(2,1)S(1)}, u32[]{:S(2)}, u32[]{:S(2)}) collective-permute-start(bf16[16,32,640]{2,1,0:T(8,128)(2,1)S(1)} %get-tuple-element.453), channel_id=1, source_target_pairs={{0,16},{1,17},{2,18},{3,19},{4,20},{5,21},{6,22},{7,23},{8,24},{9,... | collective-permute-start | bytes 1966088 | tf_op jit(solution)/shard_map/ppermute | solution.py:362
  237.6 18.2 %collective-permute-start.47 = (bf16[16,32,1408]{2,1,0:T(8,128)(2,1)S(1)}, bf16[16,32,1408]{2,1,0:T(8,128)(2,1)S(1)}, u32[]{:S(2)}, u32[]{:S(2)}) collective-permute-start(bf16[16,32,1408]{2,1,0:T(8,128)(2,1)S(1)} %get-tuple-element.452), channel_id=1, source_target_pairs={{0,2},{1,5},{2,0},{3,7},{4,6},{5,1},{6,4},{7,3},{8,10},{9,13},{10,... | collective-permute-start | bytes 4325384 | tf_op jit(solution)/shard_map/ppermute | solution.py:362
  255.7 15.0 %collective-permute-start.52 = (bf16[32,32,1536]{2,1,0:T(8,128)(2,1)S(1)}, bf16[32,32,1536]{2,1,0:T(8,128)(2,1)S(1)}, u32[]{:S(2)}, u32[]{:S(2)}) collective-permute-start(bf16[32,32,1536]{2,1,0:T(8,128)(2,1)S(1)} %get-tuple-element.486), channel_id=1, source_target_pairs={{0,1},{1,0},{2,3},{3,2},{4,5},{5,4},{6,7},{7,6},{8,9},{9,8},{10,11... | collective-permute-start | bytes 9437192 | tf_op jit(solution)/shard_map/ppermute | solution.py:362
  258.7 12.0 %collective-permute-start.53 = (bf16[32,32,640]{2,1,0:T(8,128)(2,1)S(1)}, bf16[32,32,640]{2,1,0:T(8,128)(2,1)S(1)}, u32[]{:S(2)}, u32[]{:S(2)}) collective-permute-start(bf16[32,32,640]{2,1,0:T(8,128)(2,1)S(1)} %get-tuple-element.487), channel_id=1, source_target_pairs={{0,1},{1,0},{2,3},{3,2},{4,5},{5,4},{6,7},{7,6},{8,9},{9,8},{10,11... | collective-permute-start | bytes 3932168 | tf_op jit(solution)/shard_map/ppermute | solution.py:362
  259.3 11.4 %collective-permute-start.50 = (bf16[8,32,1408]{2,1,0:T(8,128)(2,1)S(1)}, bf16[8,32,1408]{2,1,0:T(8,128)(2,1)S(1)}, u32[]{:S(2)}, u32[]{:S(2)}) collective-permute-start(bf16[8,32,1408]{2,1,0:T(8,128)(2,1)S(1)} %get-tuple-element.482), channel_id=1, source_target_pairs={{0,4},{1,17},{2,6},{3,19},{4,0},{5,21},{6,2},{7,23},{8,12},{9,25},... | collective-permute-start | bytes 2162696 | tf_op jit(solution)/shard_map/ppermute | solution.py:362
  259.4 11.4 %collective-permute-start.51 = (bf16[8,32,640]{2,1,0:T(8,128)(2,1)S(1)}, bf16[8,32,640]{2,1,0:T(8,128)(2,1)S(1)}, u32[]{:S(2)}, u32[]{:S(2)}) collective-permute-start(bf16[8,32,640]{2,1,0:T(8,128)(2,1)S(1)} %get-tuple-element.483), channel_id=1, source_target_pairs={{0,2},{1,3},{2,0},{3,1},{4,6},{5,7},{6,4},{7,5},{8,10},{9,11},{10,... | collective-permute-start | bytes 983048 | tf_op jit(solution)/shard_map/ppermute | solution.py:362
  260.0 10.7 %collective-permute-start.49 = (bf16[2,128,512]{2,1,0:T(8,128)(2,1)S(1)}, bf16[2,128,512]{2,1,0:T(8,128)(2,1)S(1)}, u32[]{:S(2)}, u32[]{:S(2)}) collective-permute-start(bf16[2,128,512]{2,1,0:T(8,128)(2,1)S(1)} %pad_maximum_fusion.6), channel_id=1, source_target_pairs={{0,8},{1,9},{2,10},{3,11},{4,12},{5,13},{6,14},{7,15},{8,0},{9,1},... | collective-permute-start | bytes 786440 | tf_op jit(solution)/shard_map/ppermute | solution.py:362
  271.9 24.9 %collective-permute-start.57 = (bf16[16,32,1536]{2,1,0:T(8,128)(2,1)S(1)}, bf16[16,32,1536]{2,1,0:T(8,128)(2,1)S(1)}, u32[]{:S(2)}, u32[]{:S(2)}) collective-permute-start(bf16[16,32,1536]{2,1,0:T(8,128)(2,1)S(1)} %get-tuple-element.508), channel_id=1, source_target_pairs={{0,2},{1,5},{2,0},{3,7},{4,6},{5,1},{6,4},{7,3},{8,10},{9,13},{10,... | collective-permute-start | bytes 4718600 | tf_op jit(solution)/shard_map/ppermute | solution.py:362
  271.9 24.8 %collective-permute-start.58 = (bf16[16,32,640]{2,1,0:T(8,128)(2,1)S(1)}, bf16[16,32,640]{2,1,0:T(8,128)(2,1)S(1)}, u32[]{:S(2)}, u32[]{:S(2)}) collective-permute-start(bf16[16,32,640]{2,1,0:T(8,128)(2,1)S(1)} %get-tuple-element.509), channel_id=1, source_target_pairs={{0,16},{1,17},{2,18},{3,19},{4,20},{5,21},{6,22},{7,23},{8,24},{9,... | collective-permute-start | bytes 1966088 | tf_op jit(solution)/shard_map/ppermute | solution.py:362
  274.3 22.4 %collective-permute-start.56 = (bf16[4,32,640]{2,1,0:T(8,128)(2,1)S(1)}, bf16[4,32,640]{2,1,0:T(8,128)(2,1)S(1)}, u32[]{:S(2)}, u32[]{:S(2)}) collective-permute-start(bf16[4,32,640]{2,1,0:T(8,128)(2,1)S(1)} %get-tuple-element.501), channel_id=1, source_target_pairs={{0,4},{1,5},{2,6},{3,7},{4,0},{5,1},{6,2},{7,3},{8,12},{9,13},{10,... | collective-permute-start | bytes 491528 | tf_op jit(solution)/shard_map/ppermute | solution.py:362
  275.8 20.9 %collective-permute-start.55 = (bf16[4,32,1408]{2,1,0:T(8,128)(2,1)S(1)}, bf16[4,32,1408]{2,1,0:T(8,128)(2,1)S(1)}, u32[]{:S(2)}, u32[]{:S(2)}) collective-permute-start(bf16[4,32,1408]{2,1,0:T(8,128)(2,1)S(1)} %get-tuple-element.500), channel_id=1, source_target_pairs={{0,16},{1,3},{2,18},{3,1},{4,20},{5,7},{6,22},{7,5},{8,24},{9,11},... | collective-permute-start | bytes 1081352 | tf_op jit(solution)/shard_map/ppermute | solution.py:362
  277.1 8.1 %collective-permute-start.54 = (bf16[128,512]{1,0:T(8,128)(2,1)S(1)}, bf16[128,512]{1,0:T(8,128)(2,1)S(1)}, u32[]{:S(2)}, u32[]{:S(2)}) collective-permute-start(bf16[128,512]{1,0:T(8,128)(2,1)S(1)} %get-tuple-element.587), channel_id=1, source_target_pairs={{0,1},{1,0},{2,3},{3,2},{4,5},{5,4},{6,7},{7,6},{8,9},{9,8},{10,11... | collective-permute-start | bytes 393224 | tf_op jit(solution)/shard_map/ppermute | solution.py:362
  297.3 11.2 %collective-permute-start.60 = (bf16[8,32,1536]{2,1,0:T(8,128)(2,1)S(1)}, bf16[8,32,1536]{2,1,0:T(8,128)(2,1)S(1)}, u32[]{:S(2)}, u32[]{:S(2)}) collective-permute-start(bf16[8,32,1536]{2,1,0:T(8,128)(2,1)S(1)} %get-tuple-element.524), channel_id=1, source_target_pairs={{0,4},{1,17},{2,6},{3,19},{4,0},{5,21},{6,2},{7,23},{8,12},{9,25},... | collective-permute-start | bytes 2359304 | tf_op jit(solution)/shard_map/ppermute | solution.py:362
  297.9 9.7 %collective-permute-start.59 = (bf16[2,32,2048]{2,1,0:T(8,128)(2,1)S(1)}, bf16[2,32,2048]{2,1,0:T(8,128)(2,1)S(1)}, u32[]{:S(2)}, u32[]{:S(2)}) collective-permute-start(bf16[2,32,2048]{2,1,0:T(8,128)(2,1)S(1)} %pad_maximum_fusion.8), channel_id=1, source_target_pairs={{0,8},{1,9},{2,10},{3,11},{4,12},{5,13},{6,14},{7,15},{8,0},{9,1},... | collective-permute-start | bytes 786440 | tf_op jit(solution)/shard_map/ppermute | solution.py:362
  299.0 8.7 %collective-permute-start.61 = (bf16[8,32,640]{2,1,0:T(8,128)(2,1)S(1)}, bf16[8,32,640]{2,1,0:T(8,128)(2,1)S(1)}, u32[]{:S(2)}, u32[]{:S(2)}) collective-permute-start(bf16[8,32,640]{2,1,0:T(8,128)(2,1)S(1)} %get-tuple-element.525), channel_id=1, source_target_pairs={{0,2},{1,3},{2,0},{3,1},{4,6},{5,7},{6,4},{7,5},{8,10},{9,11},{10,... | collective-permute-start | bytes 983048 | tf_op jit(solution)/shard_map/ppermute | solution.py:362
  308.9 13.6 %collective-permute-start.64 = (bf16[4,32,640]{2,1,0:T(8,128)(2,1)S(1)}, bf16[4,32,640]{2,1,0:T(8,128)(2,1)S(1)}, u32[]{:S(2)}, u32[]{:S(2)}) collective-permute-start(bf16[4,32,640]{2,1,0:T(8,128)(2,1)S(1)} %get-tuple-element.537), channel_id=1, source_target_pairs={{0,4},{1,5},{2,6},{3,7},{4,0},{5,1},{6,2},{7,3},{8,12},{9,13},{10,... | collective-permute-start | bytes 491528 | tf_op jit(solution)/shard_map/ppermute | solution.py:362
  309.6 12.9 %collective-permute-start.63 = (bf16[4,32,1536]{2,1,0:T(8,128)(2,1)S(1)}, bf16[4,32,1536]{2,1,0:T(8,128)(2,1)S(1)}, u32[]{:S(2)}, u32[]{:S(2)}) collective-permute-start(bf16[4,32,1536]{2,1,0:T(8,128)(2,1)S(1)} %get-tuple-element.536), channel_id=1, source_target_pairs={{0,16},{1,3},{2,18},{3,1},{4,20},{5,7},{6,22},{7,5},{8,24},{9,11},... | collective-permute-start | bytes 1179656 | tf_op jit(solution)/shard_map/ppermute | solution.py:362
  310.9 11.6 %collective-permute-start.62 = (bf16[32,2048]{1,0:T(8,128)(2,1)}, bf16[32,2048]{1,0:T(8,128)(2,1)S(1)}, u32[]{:S(2)}, u32[]{:S(2)}) collective-permute-start(bf16[32,2048]{1,0:T(8,128)(2,1)} %get-tuple-element.585), channel_id=1, source_target_pairs={{0,1},{1,0},{2,3},{3,2},{4,5},{5,4},{6,7},{7,6},{8,9},{9,8},{10,11... | collective-permute-start | bytes 393224 | tf_op jit(solution)/shard_map/ppermute | solution.py:362
  322.7 9.3 %collective-permute-start.65 = (bf16[2,32,2176]{2,1,0:T(8,128)(2,1)S(1)}, bf16[2,32,2176]{2,1,0:T(8,128)(2,1)S(1)}, u32[]{:S(2)}, u32[]{:S(2)}) collective-permute-start(bf16[2,32,2176]{2,1,0:T(8,128)(2,1)S(1)} %pad_maximum_fusion.4), channel_id=1, source_target_pairs={{0,8},{1,9},{2,10},{3,11},{4,12},{5,13},{6,14},{7,15},{8,0},{9,1},... | collective-permute-start | bytes 835592 | tf_op jit(solution)/shard_map/ppermute | solution.py:362
  324.4 7.6 %collective-permute-start.66 = (bf16[192,1024]{1,0:T(8,128)(2,1)S(1)}, bf16[192,1024]{1,0:T(8,128)(2,1)S(1)}, u32[]{:S(2)}, u32[]{:S(2)}) collective-permute-start(bf16[192,1024]{1,0:T(8,128)(2,1)S(1)} %get-tuple-element.551), channel_id=1, source_target_pairs={{0,16},{16,0},{1,17},{17,1},{2,18},{18,2},{3,19},{19,3},{4,20},{20... | collective-permute-start | bytes 1179656 | tf_op jit(solution)/shard_map/ppermute | solution.py:1106
  332.1 9.3 %collective-permute-start.67 = (bf16[32,2176]{1,0:T(8,128)(2,1)S(1)}, bf16[32,2176]{1,0:T(8,128)(2,1)S(1)}, u32[]{:S(2)}, u32[]{:S(2)}) collective-permute-start(bf16[32,2176]{1,0:T(8,128)(2,1)S(1)} %fusion.19), channel_id=1, source_target_pairs={{0,1},{1,0},{2,3},{3,2},{4,5},{5,4},{6,7},{7,6},{8,9},{9,8},{10,11... | collective-permute-start | bytes 417800 | tf_op jit(solution)/shard_map/ppermute | solution.py:362
  (39 other events, 244.7 us)
where the time goes:
time: 345 us; the launch traced here: 344 us
  waiting for transfers between devices  125 us (36%)
  Pallas kernels  80.9 us (23%)
  starting transfers between devices  73.1 us (21%)
  local copies, waits for them, and re-layouts  31.5 us (9%)
  other arithmetic  17.9 us (5%)
  matrix products  14 us (4%)
    ppermute x66, waiting for transfers between devices, swap(): return lax.ppermute(value, AXES, pairs)  125 us
    ppermute x66, starting transfers between devices, swap(): return lax.ppermute(value, AXES, pairs)  70.2 us
    pallas_call x3, Pallas kernels, gather_matmul(): pl.pallas_call(functools.partial(gather_matmul_body, routes, len(widths),...  23.5 us
    unnamed x77, local copies, waits for them, and re-layouts  15.9 us
    pallas_call x4, Pallas kernels, weight_grad(): pl.pallas_call(functools.partial(weight_grad_body, chunks, 256), out_shap...  13.5 us
    pallas_call x9, Pallas kernels, join(): pl.pallas_call(functools.partial(join_body, cut), out_shape=[jax.ShapeDty...  11.8 us
    pallas_call x1, Pallas kernels, attend_backward(): pl.pallas_call(attend_backward_body, grid=(STEPS,), in_specs=attend_specs...  9.64 us
    pallas_call x12, Pallas kernels, halve(): pl.pallas_call(halve_body, grid=(steps,), in_specs=specs, out_specs=outs,...  8.68 us
  transfers between devices with their start and end apart: 68, of which 23 were waited for; matrix products, arithmetic and copies ran while one was open for 11% of the time, Pallas kernels for 17%

commit v1 on v0

--- a/solution.py
+++ b/solution.py
@@ -622,7 +622,7 @@
 
 def halve(pairs):
     half = pairs[0][0].shape[0] // 2
-    block = max(half // 4, 1)
+    block = max(half // 2, 1)
     steps = half // block
     specs, outs, shapes, values = [], [], [], []
     for held, arrived in pairs:
@@ -1084,9 +1084,13 @@
 
     first.begin()
     inner.step()
+    row_grad, far_grad = rows_back(grad_projected, attend_mat)
+    row_grad, far_grad = sync((inner, first), row_grad, far_grad)
+
+    first.step()
+    inner.step()
     outer.step()
-    row_grad, far_grad = rows_back(grad_projected, attend_mat)
-    row_grad, far_grad = sync(movers, row_grad, far_grad)
+    sync(movers)
 
     first.step()
     inner.step()
@@ -1094,13 +1098,9 @@
     sync(movers)
 
     first.step()
-    inner.step()
+    inner.near()
     sum_outer_mat = jnp.concatenate(outer.result(), axis=1)
-    (sum_outer_mat,) = sync((inner, first), sum_outer_mat)
-
-    first.step()
-    inner.near()
-    (far_grad,) = sync((inner, first), far_grad)
+    sum_outer_mat, far_grad = sync((inner, first), sum_outer_mat, far_grad)
 
     first.step()
     far_grad = lax.ppermute(far_grad, "seq", [(0, 1), (1, 0)])

time: 345 us -> 344 us (level)
  starting transfers between devices: 73.1 us -> 50.1 us
  waiting for transfers between devices: 125 us -> 145 us
    ppermute x66, starting transfers between devices: 70.2 us -> 47.6 us  [swap(): return lax.ppermute(value, AXES, pairs)]
    ppermute x66, waiting for transfers between devices: 125 us -> 145 us  [swap(): return lax.ppermute(value, AXES, pairs)]
    unnamed x77 -> x85, local copies, waits for them, and re-layouts: 15.9 us -> 16.6 us
  transfers between devices with their start and end apart: 68 -> 68, of which waited for: 23 -> 25; matrix products, arithmetic and copies ran while one was open for 11% -> 12% of each run, Pallas kernels for 17% -> 17%
where the time goes in v1:
time: 344 us; the launch traced here: 343 us
  waiting for transfers between devices  145 us (42%)
  Pallas kernels  80.7 us (23%)
  starting transfers between devices  50.1 us (15%)
  local copies, waits for them, and re-layouts  32.1 us (9%)
  other arithmetic  19.1 us (6%)
  matrix products  13.9 us (4%)
    ppermute x66, waiting for transfers between devices, swap(): return lax.ppermute(value, AXES, pairs)  145 us
    ppermute x66, starting transfers between devices, swap(): return lax.ppermute(value, AXES, pairs)  47.6 us
    pallas_call x3, Pallas kernels, gather_matmul(): pl.pallas_call(functools.partial(gather_matmul_body, routes, len(widths),...  23.5 us
    unnamed x85, local copies, waits for them, and re-layouts  16.6 us
    pallas_call x4, Pallas kernels, weight_grad(): pl.pallas_call(functools.partial(weight_grad_body, chunks, 256), out_shap...  13.5 us
    pallas_call x9, Pallas kernels, join(): pl.pallas_call(functools.partial(join_body, cut), out_shape=[jax.ShapeDty...  11.9 us
    pallas_call x1, Pallas kernels, attend_backward(): pl.pallas_call(attend_backward_body, grid=(STEPS,), in_specs=attend_specs...  9.65 us
    pallas_call x1, Pallas kernels, attend_forward(): pl.pallas_call(attend_forward_body, grid=(STEPS,), in_specs=attend_specs(...  8.51 us
  transfers between devices with their start and end apart: 68, of which 25 were waited for; matrix products, arithmetic and copies ran while one was open for 12% of the time, Pallas kernels for 17%

profile of v1, /device:TPU:1, one launch (start us, length us, event | category | flops | bytes accessed | tf_op | source)
XLA Modules:
  0.0 342.6 jit_solution(9994796107025935956)
XLA Ops:
  6.9 3.8 %collective-permute-start.1 = (bf16[1,64,2176]{2,1,0:T(8,128)(2,1)S(1)}, bf16[1,64,2176]{2,1,0:T(8,128)(2,1)S(1)}, u32[]{:S(2)}, u32[]{:S(2)}) collective-permute-start(bf16[1,64,2176]{2,1,0:T(8,128)(2,1)S(1)} %maximum_bitcast_fusion.refs_0_), channel_id=1, source_target_pairs={{0,8},{1,9},{2,10},{3,11},{4,12},{5,13},{6,14},{7,15},{8,0},{9,1},... | collective-permute-start | bytes 835592 | tf_op jit(solution)/shard_map/ppermute | solution.py:362
  11.0 12.6 %collective-permute-done.1.refs_1_ = bf16[1,64,2176]{2,1,0:T(8,128)(2,1)S(1)} collective-permute-done((bf16[1,64,2176]{2,1,0:T(8,128)(2,1)S(1)}, bf16[1,64,2176]{2,1,0:T(8,128)(2,1)S(1)}, u32[]{:S(2)}, u32[]{:S(2)}) %collective-permute-start.1) | collective-permute-done | bytes 278560 | tf_op jit(solution)/shard_map/ppermute | solution.py:362
  24.9 1.3 collective-permute-start.4
  26.4 3.9 %collective-permute-start.5 = (bf16[2,64,640]{2,1,0:T(8,128)(2,1)S(1)}, bf16[2,64,640]{2,1,0:T(8,128)(2,1)S(1)}, u32[]{:S(2)}, u32[]{:S(2)}) collective-permute-start(bf16[2,64,640]{2,1,0:T(8,128)(2,1)S(1)} %get-tuple-element.297.refs_2_), channel_id=1, source_target_pairs={{0,4},{1,5},{2,6},{3,7},{4,0},{5,1},{6,2},{7,3},{8,12},{9,13},{10,... | collective-permute-start | bytes 491528 | tf_op jit(solution)/shard_map/ppermute | solution.py:362
  30.2 5.3 %collective-permute-done.5.refs_3_ = bf16[2,64,640]{2,1,0:T(8,128)(2,1)S(1)} collective-permute-done((bf16[2,64,640]{2,1,0:T(8,128)(2,1)S(1)}, bf16[2,64,640]{2,1,0:T(8,128)(2,1)S(1)}, u32[]{:S(2)}, u32[]{:S(2)}) %collective-permute-start.5) | collective-permute-done | bytes 163872 | tf_op jit(solution)/shard_map/ppermute | solution.py:362
  35.6 4.8 %collective-permute-done.6.refs_1_ = bf16[1,64,2048]{2,1,0:T(8,128)(2,1)S(1)} collective-permute-done((bf16[1,64,2048]{2,1,0:T(8,128)(2,1)S(1)}, bf16[1,64,2048]{2,1,0:T(8,128)(2,1)S(1)}, u32[]{:S(2)}, u32[]{:S(2)}) %collective-permute-start.6) | collective-permute-done | bytes 262176 | tf_op jit(solution)/shard_map/ppermute | solution.py:362
  41.6 7.8 %collective-permute-done.9.refs_3_ = bf16[4,64,640]{2,1,0:T(8,128)(2,1)S(1)} collective-permute-done((bf16[4,64,640]{2,1,0:T(8,128)(2,1)S(1)}, bf16[4,64,640]{2,1,0:T(8,128)(2,1)S(1)}, u32[]{:S(2)}, u32[]{:S(2)}) %collective-permute-start.9) | collective-permute-done | bytes 327712 | tf_op jit(solution)/shard_map/ppermute | solution.py:362
  49.4 3.0 collective-permute-done.8.refs_1_
  53.4 2.0 collective-permute-start.14
  55.4 22.2 %collective-permute-done.14.refs_1_ = bf16[1,256,512]{2,1,0:T(8,128)(2,1)S(1)} collective-permute-done((bf16[1,256,512]{2,1,0:T(8,128)(2,1)S(1)}, bf16[1,256,512]{2,1,0:T(8,128)(2,1)S(1)}, u32[]{:S(2)}, u32[]{:S(2)}) %collective-permute-start.14) | collective-permute-done | bytes 262176 | tf_op jit(solution)/shard_map/ppermute | solution.py:362
  77.6 3.7 %collective-permute-done.13.refs_3_ = bf16[2,64,640]{2,1,0:T(8,128)(2,1)S(1)} collective-permute-done((bf16[2,64,640]{2,1,0:T(8,128)(2,1)S(1)}, bf16[2,64,640]{2,1,0:T(8,128)(2,1)S(1)}, u32[]{:S(2)}, u32[]{:S(2)}) %collective-permute-start.13) | collective-permute-done | bytes 163872 | tf_op jit(solution)/shard_map/ppermute | solution.py:362
  82.4 1.7 shard_map.275
  85.0 2.9 collective-permute-done.20.refs_7_
  89.1 9.8 %shard_map.277 = (bf16[1024,3072]{1,0:T(8,128)(2,1)}, bf16[1024,1024]{1,0:T(8,128)(2,1)S(1)}, bf16[1024,256]{1,0:T(8,128)(2,1)S(1)}, f32[448,3072]{1,0:T(8,128)}) custom-call(s32[1]{0:T(128)} %bitcast.16.me_ref, bf16[448,1024]{1,0:T(8,128)(2,1)S(1)} %pad_maximum_fusion.left_ref, bf16[8,64,1536]{2,1,0:T(8,128)(2,1)S(1)} %get-tuple-element.331.refs_0_, ...), custom_call_target="tpu_custom_call" | custom-call | flops 1 | bytes 1 | tf_op jit(solution)/shard_map/pallas_call | solution.py:517
  98.9 1.3 copy-done.8
  100.2 1.4 slice_reduce_fusion.1
  101.8 3.2 add_convert_fusion.query_ref.key_ref.value_ref
  105.0 3.0 shard_map.278
  108.0 1.4 collective-permute-start.25
  110.0 2.1 shard_map.279
  112.2 1.5 collective-permute-start.26
  114.0 8.5 %shard_map.280 = (bf16[256,1024]{1,0:T(8,128)(2,1)S(1)}, f32[8,2,256]{2,1,0:T(2,128)S(1)}) custom-call(s32[1,256]{1,0:T(1,128)S(1)} %bitcast.115, s32[448,1]{1,0:T(8,128)S(1)} %copy.37.key_docs, bf16[448,3072]{1,0:T(8,128)(2,1)S(1)} %add_convert_fusion.query_ref.key_ref.value_ref, bf16[448,3072]{1,0:T(8,128)(2,1)S(1)} %add_convert_fusion.query_ref.key_ref.value_ref, ...), custom_call_target="tpu_custom_call" | custom-call | flops 1 | bytes 1 | tf_op jit(solution)/shard_map/pallas_call | solution.py:800
  125.7 1.6 copy-done.9
  128.4 1.4 shard_map.281
  133.2 4.3 %collective-permute-done.24.refs_3_ = bf16[8,64,640]{2,1,0:T(8,128)(2,1)} collective-permute-done((bf16[8,64,640]{2,1,0:T(8,128)(2,1)}, bf16[8,64,640]{2,1,0:T(8,128)(2,1)}, u32[]{:S(2)}, u32[]{:S(2)}) %collective-permute-start.24) | collective-permute-done | bytes 655392 | tf_op jit(solution)/shard_map/ppermute | solution.py:362
  138.1 2.8 shard_map.282
  142.2 1.5 slice.176
  144.8 1.5 collective-permute-start.29
  147.3 7.1 %shard_map.283 = (bf16[1024,4096]{1,0:T(8,128)(2,1)}, f32[256,4096]{1,0:T(8,128)S(1)}) custom-call(s32[1]{0:T(128)} %bitcast.16.me_ref, bf16[256,1024]{1,0:T(8,128)(2,1)S(1)} %copy-done.15, bf16[8,64,1408]{2,1,0:T(8,128)(2,1)} %get-tuple-element.375.refs_0_, bf16[8,64,640]{2,1,0:T(8,128)(2,1)} %get-tuple-element.376.refs_1_, ...), custom_call_target="tpu_custom_call" | custom-call | flops 1 | bytes 1 | tf_op jit(solution)/shard_map/pallas_call | solution.py:517
  154.5 3.6 %fusion.4 = (f32[256,4096]{1,0:T(8,128)}, bf16[256,4096]{1,0:T(8,128)(2,1)}) fusion(f32[256,4096]{1,0:T(8,128)S(1)} %get-tuple-element.383, f32[4096]{0:T(1024)S(1)} %add.166), kind=kLoop, calls=%fused_computation.7 | loop fusion | flops 11534336 | bytes 10502144 | tf_op jit(solution)/shard_map/add | solution.py:1016
  158.9 2.4 collective-permute-done.28.refs_2_
  164.6 1.8 collective-permute-done.36.refs_7_
  166.3 1.6 copy-done
  169.0 6.6 %shard_map.284 = (bf16[4096,1024]{1,0:T(8,128)(2,1)}, f32[256,1024]{1,0:T(8,128)S(1)}) custom-call(s32[1]{0:T(128)} %bitcast.16.me_ref, bf16[256,4096]{1,0:T(8,128)(2,1)S(1)} %copy-done, bf16[8,256,384]{2,1,0:T(8,128)(2,1)} %get-tuple-element.385.refs_0_, bf16[8,256,128]{2,1,0:T(8,128)(2,1)S(1)} %get-tuple-element.386.refs_1_, ...), custom_call_target="tpu_custom_call" | custom-call | flops 1 | bytes 1 | tf_op jit(solution)/shard_map/pallas_call | solution.py:517
  177.0 1.6 fusion.24
  178.6 5.8 %shard_map.285 = (bf16[32,128,384]{2,1,0:T(8,128)(2,1)S(1)}, bf16[32,128,384]{2,1,0:T(8,128)(2,1)}, bf16[32,128,128]{2,1,0:T(8,128)(2,1)S(1)}, bf16[32,128,128]{2,1,0:T(8,128)(2,1)}) custom-call(s32[1]{0:T(128)} %bitcast.16.me_ref, bf16[256,4096]{1,0:T(8,128)(2,1)S(1)} %copy-done, bf16[256,1024]{1,0:T(8,128)(2,1)S(1)} %get-tuple-element.421.right_ref), custom_call_target="tpu_custom_call" | custom-call | flops 1 | bytes 1 | tf_op jit(solution)/shard_map/pallas_call | solution.py:598
  184.4 1.6 copy-done.1
  188.8 7.1 %convert_reduce_fusion = (bf16[4096]{0:T(1024)(128)(2,1)S(1)}, bf16[256,4096]{1,0:T(8,128)(2,1)S(1)}) fusion(f32[256,4096]{1,0:T(8,128)} %get-tuple-element.402, bf16[256,1024]{1,0:T(8,128)(2,1)S(1)} %get-tuple-element.421.right_ref, bf16[4096,1024]{1,0:T(8,128)(2,1)} %get-tuple-element.401), kind=kOutput, calls=%fused_computation.8 | convolution fusion | flops 2151673856 | bytes 15212544 | tf_op jit(solution)/shard_map/td,fd->tf/dot_general | solution.py:1036
  195.9 2.8 shard_map.286
  198.8 1.5 collective-permute-start.40
  201.1 6.1 %multiply_reduce_fusion = (bf16[1024]{0:T(1024)(128)(2,1)S(1)}, f32[256]{0:T(256)S(1)}, f32[256]{0:T(256)S(1)}, bf16[1024]{0:T(1024)(128)(2,1)S(1)}, f32[256,1024]{1,0:T(8,128)S(1)}) fusion(f32[256,1024]{1,0:T(8,128)S(1)} %copy-done.22, f32[1024]{0:T(1024)S(1)} %mul.180, f32[256,1024]{1,0:T(8,128)S(1)} %copy-done.32, ...), kind=kOutput, calls=%fused_computation.26 | convolution fusion | flops 2149578240 | bytes 13641728 | tf_op jit(solution)/shard_map/tf,df->td/dot_general | solution.py:1051
  208.6 3.0 shard_map.287
  212.6 7.2 %collective-permute-done.39.refs_2_.refs_3_ = bf16[16,128,384]{2,1,0:T(8,128)(2,1)S(1)} collective-permute-done((bf16[16,128,384]{2,1,0:T(8,128)(2,1)S(1)}, bf16[16,128,384]{2,1,0:T(8,128)(2,1)S(1)}, u32[]{:S(2)}, u32[]{:S(2)}) %collective-permute-start.39) | collective-permute-done | bytes 1572896 | tf_op jit(solution)/shard_map/ppermute | solution.py:362
  219.8 1.5 collective-permute-start.43
  222.2 9.6 %shard_map.289 = (bf16[448,3072]{1,0:T(8,128)(2,1)S(1)}, f32[2,1,1024]{2,1,0:T(1,128)S(1)}) custom-call(s32[1,256]{1,0:T(1,128)S(1)} %bitcast.116, s32[448,1]{1,0:T(8,128)S(1)} %copy.37.key_docs, bf16[448,3072]{1,0:T(8,128)(2,1)S(1)} %add_convert_fusion.query_ref.key_ref.value_ref, bf16[448,3072]{1,0:T(8,128)(2,1)S(1)} %add_convert_fusion.query_ref.key_ref.value_ref, ...), custom_call_target="tpu_custom_call" | custom-call | flops 1 | bytes 1 | tf_op jit(solution)/shard_map/pallas_call | solution.py:866
  235.4 1.5 collective-permute-start.48
  237.6 3.8 %shard_map.292 = (bf16[32,32,1536]{2,1,0:T(8,128)(2,1)S(1)}, bf16[32,32,1536]{2,1,0:T(8,128)(2,1)S(1)}) custom-call(s32[1]{0:T(128)} %bitcast.16.me_ref, bf16[448,1024]{1,0:T(8,128)(2,1)S(1)} %copy-done.4, bf16[448,3072]{1,0:T(8,128)(2,1)S(1)} %get-tuple-element.456.right_ref.grad_ref), custom_call_target="tpu_custom_call" | custom-call | flops 1 | bytes 1 | tf_op jit(solution)/shard_map/pallas_call | solution.py:598
  242.4 8.9 %collective-permute-done.48.refs_6_.refs_7_ = bf16[16,32,640]{2,1,0:T(8,128)(2,1)S(1)} collective-permute-done((bf16[16,32,640]{2,1,0:T(8,128)(2,1)S(1)}, bf16[16,32,640]{2,1,0:T(8,128)(2,1)S(1)}, u32[]{:S(2)}, u32[]{:S(2)}) %collective-permute-start.48) | collective-permute-done | bytes 655392 | tf_op jit(solution)/shard_map/ppermute | solution.py:362
  251.4 3.7 %collective-permute-done.47.refs_2_.refs_3_ = bf16[16,32,1408]{2,1,0:T(8,128)(2,1)S(1)} collective-permute-done((bf16[16,32,1408]{2,1,0:T(8,128)(2,1)S(1)}, bf16[16,32,1408]{2,1,0:T(8,128)(2,1)S(1)}, u32[]{:S(2)}, u32[]{:S(2)}) %collective-permute-start.47) | collective-permute-done | bytes 1441824 | tf_op jit(solution)/shard_map/ppermute | solution.py:362
  255.1 3.0 collective-permute-start.51
  259.2 3.7 %shard_map.295 = (f32[256,1024]{1,0:T(8,128)S(1)}, bf16[192,1024]{1,0:T(8,128)(2,1)S(1)}) custom-call(bf16[448,3072]{1,0:T(8,128)(2,1)S(1)} %get-tuple-element.456.right_ref.grad_ref, bf16[1024,3072]{1,0:T(8,128)(2,1)S(1)} %bitcast.110), custom_call_target="tpu_custom_call" | custom-call | flops 1 | bytes 1 | tf_op jit(solution)/shard_map/pallas_call | solution.py:693
  262.9 3.7 %collective-permute-done.50.refs_6_.refs_7_ = bf16[8,32,640]{2,1,0:T(8,128)(2,1)S(1)} collective-permute-done((bf16[8,32,640]{2,1,0:T(8,128)(2,1)S(1)}, bf16[8,32,640]{2,1,0:T(8,128)(2,1)S(1)}, u32[]{:S(2)}, u32[]{:S(2)}) %collective-permute-start.50) | collective-permute-done | bytes 327712 | tf_op jit(solution)/shard_map/ppermute | solution.py:362
  266.6 2.5 collective-permute-done.49.refs_2_.refs_3_
  274.9 20.7 %collective-permute-done.53 = bf16[2,128,512]{2,1,0:T(8,128)(2,1)S(1)} collective-permute-done((bf16[2,128,512]{2,1,0:T(8,128)(2,1)S(1)}, bf16[2,128,512]{2,1,0:T(8,128)(2,1)S(1)}, u32[]{:S(2)}, u32[]{:S(2)}) %collective-permute-start.53) | collective-permute-done | bytes 262176 | tf_op jit(solution)/shard_map/ppermute | solution.py:362
  295.6 3.0 collective-permute-done.55.refs_6_.refs_7_
  304.0 1.3 collective-permute-done.58
  305.3 5.9 %collective-permute-done.59 = bf16[2,32,2048]{2,1,0:T(8,128)(2,1)S(1)} collective-permute-done((bf16[2,32,2048]{2,1,0:T(8,128)(2,1)S(1)}, bf16[2,32,2048]{2,1,0:T(8,128)(2,1)S(1)}, u32[]{:S(2)}, u32[]{:S(2)}) %collective-permute-start.59) | collective-permute-done | bytes 262176 | tf_op jit(solution)/shard_map/ppermute | solution.py:362
  312.8 3.6 %collective-permute-start.62 = (bf16[32,2048]{1,0:T(8,128)(2,1)S(1)}, bf16[32,2048]{1,0:T(8,128)(2,1)S(1)}, u32[]{:S(2)}, u32[]{:S(2)}) collective-permute-start(bf16[32,2048]{1,0:T(8,128)(2,1)S(1)} %get-tuple-element.585), channel_id=1, source_target_pairs={{0,1},{1,0},{2,3},{3,2},{4,5},{5,4},{6,7},{7,6},{8,9},{9,8},{10,11... | collective-permute-start | bytes 393224 | tf_op jit(solution)/shard_map/ppermute | solution.py:362
  316.4 1.3 collective-permute-start.64
  318.6 3.6 %collective-permute-done.64.refs_6_.refs_7_ = bf16[4,32,640]{2,1,0:T(8,128)(2,1)S(1)} collective-permute-done((bf16[4,32,640]{2,1,0:T(8,128)(2,1)S(1)}, bf16[4,32,640]{2,1,0:T(8,128)(2,1)S(1)}, u32[]{:S(2)}, u32[]{:S(2)}) %collective-permute-start.64) | collective-permute-done | bytes 163872 | tf_op jit(solution)/shard_map/ppermute | solution.py:362
  322.4 1.6 collective-permute-start.65
  324.0 1.4 collective-permute-start.66
  326.4 10.5 %collective-permute-done.65 = bf16[2,32,2176]{2,1,0:T(8,128)(2,1)S(1)} collective-permute-done((bf16[2,32,2176]{2,1,0:T(8,128)(2,1)S(1)}, bf16[2,32,2176]{2,1,0:T(8,128)(2,1)S(1)}, u32[]{:S(2)}, u32[]{:S(2)}) %collective-permute-start.65) | collective-permute-done | bytes 278560 | tf_op jit(solution)/shard_map/ppermute | solution.py:362
  336.9 1.6 collective-permute-start.67
  (280 shorter events, 64.1 us)
Async XLA Ops:
  5.2 5.8 %collective-permute-start.3 = (bf16[128,512]{1,0:T(8,128)(2,1)S(1)}, bf16[128,512]{1,0:T(8,128)(2,1)S(1)}, u32[]{:S(2)}, u32[]{:S(2)}) collective-permute-start(bf16[128,512]{1,0:T(8,128)(2,1)S(1)} %get-tuple-element.599), channel_id=1, source_target_pairs={{0,1},{1,0},{2,3},{3,2},{4,5},{5,4},{6,7},{7,6},{8,9},{9,8},{10,11... | collective-permute-start | bytes 393224 | tf_op jit(solution)/shard_map/ppermute | solution.py:362
  6.7 4.3 %collective-permute-start.2 = (bf16[32,2048]{1,0:T(8,128)(2,1)S(1)}, bf16[32,2048]{1,0:T(8,128)(2,1)S(1)}, u32[]{:S(2)}, u32[]{:S(2)}) collective-permute-start(bf16[32,2048]{1,0:T(8,128)(2,1)S(1)} %get-tuple-element.601), channel_id=1, source_target_pairs={{0,1},{1,0},{2,3},{3,2},{4,5},{5,4},{6,7},{7,6},{8,9},{9,8},{10,11... | collective-permute-start | bytes 393224 | tf_op jit(solution)/shard_map/ppermute | solution.py:362
  6.9 16.8 %collective-permute-start.1 = (bf16[1,64,2176]{2,1,0:T(8,128)(2,1)S(1)}, bf16[1,64,2176]{2,1,0:T(8,128)(2,1)S(1)}, u32[]{:S(2)}, u32[]{:S(2)}) collective-permute-start(bf16[1,64,2176]{2,1,0:T(8,128)(2,1)S(1)} %maximum_bitcast_fusion.refs_0_), channel_id=1, source_target_pairs={{0,8},{1,9},{2,10},{3,11},{4,12},{5,13},{6,14},{7,15},{8,0},{9,1},... | collective-permute-start | bytes 835592 | tf_op jit(solution)/shard_map/ppermute | solution.py:362
  23.7 16.7 %collective-permute-start.7 = (bf16[192,1024]{1,0:T(8,128)(2,1)S(1)}, bf16[192,1024]{1,0:T(8,128)(2,1)S(1)}, u32[]{:S(2)}, u32[]{:S(2)}) collective-permute-start(bf16[192,1024]{1,0:T(8,128)(2,1)S(1)} %constant_dynamic-slice_fusion.1), channel_id=1, source_target_pairs={{0,16},{16,0},{1,17},{17,1},{2,18},{18,2},{3,19},{19,3},{4,20},{20... | collective-permute-start | bytes 1179656 | tf_op jit(solution)/shard_map/ppermute | solution.py:958
  24.9 15.5 %collective-permute-start.4 = (bf16[2,64,1536]{2,1,0:T(8,128)(2,1)S(1)}, bf16[2,64,1536]{2,1,0:T(8,128)(2,1)S(1)}, u32[]{:S(2)}, u32[]{:S(2)}) collective-permute-start(bf16[2,64,1536]{2,1,0:T(8,128)(2,1)S(1)} %get-tuple-element.295.refs_0_), channel_id=1, source_target_pairs={{0,16},{1,3},{2,18},{3,1},{4,20},{5,7},{6,22},{7,5},{8,24},{9,11},... | collective-permute-start | bytes 1179656 | tf_op jit(solution)/shard_map/ppermute | solution.py:362
  26.3 14.1 %collective-permute-start.6 = (bf16[1,64,2048]{2,1,0:T(8,128)(2,1)S(1)}, bf16[1,64,2048]{2,1,0:T(8,128)(2,1)S(1)}, u32[]{:S(2)}, u32[]{:S(2)}) collective-permute-start(bf16[1,64,2048]{2,1,0:T(8,128)(2,1)S(1)} %maximum_bitcast_fusion.1.refs_0_), channel_id=1, source_target_pairs={{0,8},{1,9},{2,10},{3,11},{4,12},{5,13},{6,14},{7,15},{8,0},{9,1},... | collective-permute-start | bytes 786440 | tf_op jit(solution)/shard_map/ppermute | solution.py:362
  26.4 9.2 %collective-permute-start.5 = (bf16[2,64,640]{2,1,0:T(8,128)(2,1)S(1)}, bf16[2,64,640]{2,1,0:T(8,128)(2,1)S(1)}, u32[]{:S(2)}, u32[]{:S(2)}) collective-permute-start(bf16[2,64,640]{2,1,0:T(8,128)(2,1)S(1)} %get-tuple-element.297.refs_2_), channel_id=1, source_target_pairs={{0,4},{1,5},{2,6},{3,7},{4,0},{5,1},{6,2},{7,3},{8,12},{9,13},{10,... | collective-permute-start | bytes 491528 | tf_op jit(solution)/shard_map/ppermute | solution.py:362
  41.2 11.2 %collective-permute-start.8 = (bf16[4,64,1536]{2,1,0:T(8,128)(2,1)S(1)}, bf16[4,64,1536]{2,1,0:T(8,128)(2,1)S(1)}, u32[]{:S(2)}, u32[]{:S(2)}) collective-permute-start(bf16[4,64,1536]{2,1,0:T(8,128)(2,1)S(1)} %get-tuple-element.304.refs_0_), channel_id=1, source_target_pairs={{0,4},{1,17},{2,6},{3,19},{4,0},{5,21},{6,2},{7,23},{8,12},{9,25},... | collective-permute-start | bytes 2359304 | tf_op jit(solution)/shard_map/ppermute | solution.py:362
  41.3 8.1 %collective-permute-start.9 = (bf16[4,64,640]{2,1,0:T(8,128)(2,1)S(1)}, bf16[4,64,640]{2,1,0:T(8,128)(2,1)S(1)}, u32[]{:S(2)}, u32[]{:S(2)}) collective-permute-start(bf16[4,64,640]{2,1,0:T(8,128)(2,1)S(1)} %get-tuple-element.306.refs_2_), channel_id=1, source_target_pairs={{0,2},{1,3},{2,0},{3,1},{4,6},{5,7},{6,4},{7,5},{8,10},{9,11},{10,... | collective-permute-start | bytes 983048 | tf_op jit(solution)/shard_map/ppermute | solution.py:362
  52.8 28.5 %collective-permute-start.10 = (bf16[8,64,1536]{2,1,0:T(8,128)(2,1)S(1)}, bf16[8,64,1536]{2,1,0:T(8,128)(2,1)S(1)}, u32[]{:S(2)}, u32[]{:S(2)}) collective-permute-start(bf16[8,64,1536]{2,1,0:T(8,128)(2,1)S(1)} %get-tuple-element.331.refs_0_), channel_id=1, source_target_pairs={{0,2},{1,5},{2,0},{3,7},{4,6},{5,1},{6,4},{7,3},{8,10},{9,13},{10,... | collective-permute-start | bytes 4718600 | tf_op jit(solution)/shard_map/ppermute | solution.py:362
  52.9 28.4 %collective-permute-start.11 = (bf16[8,64,640]{2,1,0:T(8,128)(2,1)S(1)}, bf16[8,64,640]{2,1,0:T(8,128)(2,1)S(1)}, u32[]{:S(2)}, u32[]{:S(2)}) collective-permute-start(bf16[8,64,640]{2,1,0:T(8,128)(2,1)S(1)} %get-tuple-element.332.refs_1_), channel_id=1, source_target_pairs={{0,16},{1,17},{2,18},{3,19},{4,20},{5,21},{6,22},{7,23},{8,24},{9,... | collective-permute-start | bytes 1966088 | tf_op jit(solution)/shard_map/ppermute | solution.py:362
  53.1 28.1 %collective-permute-start.12 = (bf16[2,64,1408]{2,1,0:T(8,128)(2,1)S(1)}, bf16[2,64,1408]{2,1,0:T(8,128)(2,1)S(1)}, u32[]{:S(2)}, u32[]{:S(2)}) collective-permute-start(bf16[2,64,1408]{2,1,0:T(8,128)(2,1)S(1)} %get-tuple-element.316.refs_0_), channel_id=1, source_target_pairs={{0,16},{1,3},{2,18},{3,1},{4,20},{5,7},{6,22},{7,5},{8,24},{9,11},... | collective-permute-start | bytes 1081352 | tf_op jit(solution)/shard_map/ppermute | solution.py:362
  53.4 24.2 %collective-permute-start.14 = (bf16[1,256,512]{2,1,0:T(8,128)(2,1)S(1)}, bf16[1,256,512]{2,1,0:T(8,128)(2,1)S(1)}, u32[]{:S(2)}, u32[]{:S(2)}) collective-permute-start(bf16[1,256,512]{2,1,0:T(8,128)(2,1)S(1)} %maximum_bitcast_fusion.2.refs_0_), channel_id=1, source_target_pairs={{0,8},{1,9},{2,10},{3,11},{4,12},{5,13},{6,14},{7,15},{8,0},{9,1},... | collective-permute-start | bytes 786440 | tf_op jit(solution)/shard_map/ppermute | solution.py:362
  55.3 25.9 %collective-permute-start.13 = (bf16[2,64,640]{2,1,0:T(8,128)(2,1)S(1)}, bf16[2,64,640]{2,1,0:T(8,128)(2,1)S(1)}, u32[]{:S(2)}, u32[]{:S(2)}) collective-permute-start(bf16[2,64,640]{2,1,0:T(8,128)(2,1)S(1)} %get-tuple-element.318.refs_2_), channel_id=1, source_target_pairs={{0,4},{1,5},{2,6},{3,7},{4,0},{5,1},{6,2},{7,3},{8,12},{9,13},{10,... | collective-permute-start | bytes 491528 | tf_op jit(solution)/shard_map/ppermute | solution.py:362
  81.3 7.6 %collective-permute-start.19 = (bf16[8,64,1536]{2,1,0:T(8,128)(2,1)S(1)}, bf16[8,64,1536]{2,1,0:T(8,128)(2,1)S(1)}, u32[]{:S(2)}, u32[]{:S(2)}) collective-permute-start(bf16[8,64,1536]{2,1,0:T(8,128)(2,1)S(1)} %collective-permute-done.10.refs_2_), channel_id=1, source_target_pairs={{0,1},{1,0},{2,3},{3,2},{4,5},{5,4},{6,7},{7,6},{8,9},{9,8},{10,11... | collective-permute-start | bytes 4718600 | tf_op jit(solution)/shard_map/ppermute | solution.py:362
  81.4 7.7 %collective-permute-start.21 = (bf16[8,64,1536]{2,1,0:T(8,128)(2,1)S(1)}, bf16[8,64,1536]{2,1,0:T(8,128)(2,1)S(1)}, u32[]{:S(2)}, u32[]{:S(2)}) collective-permute-start(bf16[8,64,1536]{2,1,0:T(8,128)(2,1)S(1)} %get-tuple-element.331.refs_0_), channel_id=1, source_target_pairs={{0,1},{1,0},{2,3},{3,2},{4,5},{5,4},{6,7},{7,6},{8,9},{9,8},{10,11... | collective-permute-start | bytes 4718600 | tf_op jit(solution)/shard_map/ppermute | solution.py:362
  81.9 6.1 %collective-permute-start.20 = (bf16[8,64,640]{2,1,0:T(8,128)(2,1)S(1)}, bf16[8,64,640]{2,1,0:T(8,128)(2,1)S(1)}, u32[]{:S(2)}, u32[]{:S(2)}) collective-permute-start(bf16[8,64,640]{2,1,0:T(8,128)(2,1)S(1)} %collective-permute-done.11.refs_3_), channel_id=1, source_target_pairs={{0,1},{1,0},{2,3},{3,2},{4,5},{5,4},{6,7},{7,6},{8,9},{9,8},{10,11... | collective-permute-start | bytes 1966088 | tf_op jit(solution)/shard_map/ppermute | solution.py:362
  81.9 6.9 %collective-permute-start.22 = (bf16[8,64,640]{2,1,0:T(8,128)(2,1)S(1)}, bf16[8,64,640]{2,1,0:T(8,128)(2,1)S(1)}, u32[]{:S(2)}, u32[]{:S(2)}) collective-permute-start(bf16[8,64,640]{2,1,0:T(8,128)(2,1)S(1)} %get-tuple-element.332.refs_1_), channel_id=1, source_target_pairs={{0,1},{1,0},{2,3},{3,2},{4,5},{5,4},{6,7},{7,6},{8,9},{9,8},{10,11... | collective-permute-start | bytes 1966088 | tf_op jit(solution)/shard_map/ppermute | solution.py:362
  84.1 20.9 %collective-permute-start.16 = (bf16[4,64,640]{2,1,0:T(8,128)(2,1)}, bf16[4,64,640]{2,1,0:T(8,128)(2,1)}, u32[]{:S(2)}, u32[]{:S(2)}) collective-permute-start(bf16[4,64,640]{2,1,0:T(8,128)(2,1)} %get-tuple-element.343.refs_2_), channel_id=1, source_target_pairs={{0,2},{1,3},{2,0},{3,1},{4,6},{5,7},{6,4},{7,5},{8,10},{9,11},{10,... | collective-permute-start | bytes 983048 | tf_op jit(solution)/shard_map/ppermute | solution.py:362
  87.9 17.0 %collective-permute-start.18 = (bf16[2,256,128]{2,1,0:T(8,128)(2,1)S(1)}, bf16[2,256,128]{2,1,0:T(8,128)(2,1)S(1)}, u32[]{:S(2)}, u32[]{:S(2)}) collective-permute-start(bf16[2,256,128]{2,1,0:T(8,128)(2,1)S(1)} %get-tuple-element.349.refs_2_), channel_id=1, source_target_pairs={{0,4},{1,5},{2,6},{3,7},{4,0},{5,1},{6,2},{7,3},{8,12},{9,13},{10,... | collective-permute-start | bytes 393224 | tf_op jit(solution)/shard_map/ppermute | solution.py:362
  88.9 16.1 %collective-permute-start.17 = (bf16[2,256,384]{2,1,0:T(8,128)(2,1)}, bf16[2,256,384]{2,1,0:T(8,128)(2,1)}, u32[]{:S(2)}, u32[]{:S(2)}) collective-permute-start(bf16[2,256,384]{2,1,0:T(8,128)(2,1)} %get-tuple-element.347.refs_0_), channel_id=1, source_target_pairs={{0,16},{1,3},{2,18},{3,1},{4,20},{5,7},{6,22},{7,5},{8,24},{9,11},... | collective-permute-start | bytes 1179656 | tf_op jit(solution)/shard_map/ppermute | solution.py:362
  88.9 16.1 %collective-permute-start.15 = (bf16[4,64,1408]{2,1,0:T(8,128)(2,1)}, bf16[4,64,1408]{2,1,0:T(8,128)(2,1)}, u32[]{:S(2)}, u32[]{:S(2)}) collective-permute-start(bf16[4,64,1408]{2,1,0:T(8,128)(2,1)} %get-tuple-element.341.refs_0_), channel_id=1, source_target_pairs={{0,4},{1,17},{2,6},{3,19},{4,0},{5,21},{6,2},{7,23},{8,12},{9,25},... | collective-permute-start | bytes 2162696 | tf_op jit(solution)/shard_map/ppermute | solution.py:362
  108.0 29.5 %collective-permute-start.25 = (bf16[8,64,1408]{2,1,0:T(8,128)(2,1)}, bf16[8,64,1408]{2,1,0:T(8,128)(2,1)}, u32[]{:S(2)}, u32[]{:S(2)}) collective-permute-start(bf16[8,64,1408]{2,1,0:T(8,128)(2,1)} %get-tuple-element.375.refs_0_), channel_id=1, source_target_pairs={{0,1},{1,0},{2,3},{3,2},{4,5},{5,4},{6,7},{7,6},{8,9},{9,8},{10,11... | collective-permute-start | bytes 4325384 | tf_op jit(solution)/shard_map/ppermute | solution.py:362
  109.4 28.1 %collective-permute-start.23 = (bf16[8,64,1408]{2,1,0:T(8,128)(2,1)}, bf16[8,64,1408]{2,1,0:T(8,128)(2,1)}, u32[]{:S(2)}, u32[]{:S(2)}) collective-permute-start(bf16[8,64,1408]{2,1,0:T(8,128)(2,1)} %get-tuple-element.375.refs_0_), channel_id=1, source_target_pairs={{0,2},{1,5},{2,0},{3,7},{4,6},{5,1},{6,4},{7,3},{8,10},{9,13},{10,... | collective-permute-start | bytes 4325384 | tf_op jit(solution)/shard_map/ppermute | solution.py:362
  112.2 25.3 %collective-permute-start.26 = (bf16[4,256,384]{2,1,0:T(8,128)(2,1)}, bf16[4,256,384]{2,1,0:T(8,128)(2,1)}, u32[]{:S(2)}, u32[]{:S(2)}) collective-permute-start(bf16[4,256,384]{2,1,0:T(8,128)(2,1)} %get-tuple-element.363.refs_0_), channel_id=1, source_target_pairs={{0,4},{1,17},{2,6},{3,19},{4,0},{5,21},{6,2},{7,23},{8,12},{9,25},... | collective-permute-start | bytes 2359304 | tf_op jit(solution)/shard_map/ppermute | solution.py:362
  113.7 23.7 %collective-permute-start.24 = (bf16[8,64,640]{2,1,0:T(8,128)(2,1)}, bf16[8,64,640]{2,1,0:T(8,128)(2,1)}, u32[]{:S(2)}, u32[]{:S(2)}) collective-permute-start(bf16[8,64,640]{2,1,0:T(8,128)(2,1)} %get-tuple-element.376.refs_1_), channel_id=1, source_target_pairs={{0,16},{1,17},{2,18},{3,19},{4,20},{5,21},{6,22},{7,23},{8,24},{9,... | collective-permute-start | bytes 1966088 | tf_op jit(solution)/shard_map/ppermute | solution.py:362
  113.8 19.4 %collective-permute-start.27 = (bf16[4,256,128]{2,1,0:T(8,128)(2,1)}, bf16[4,256,128]{2,1,0:T(8,128)(2,1)}, u32[]{:S(2)}, u32[]{:S(2)}) collective-permute-start(bf16[4,256,128]{2,1,0:T(8,128)(2,1)} %get-tuple-element.365.refs_2_), channel_id=1, source_target_pairs={{0,2},{1,3},{2,0},{3,1},{4,6},{5,7},{6,4},{7,5},{8,10},{9,11},{10,... | collective-permute-start | bytes 786440 | tf_op jit(solution)/shard_map/ppermute | solution.py:362
  137.5 8.8 %collective-permute-start.32 = (bf16[8,64,1408]{2,1,0:T(8,128)(2,1)}, bf16[8,64,1408]{2,1,0:T(8,128)(2,1)}, u32[]{:S(2)}, u32[]{:S(2)}) collective-permute-start(bf16[8,64,1408]{2,1,0:T(8,128)(2,1)} %collective-permute-done.23.refs_2_), channel_id=1, source_target_pairs={{0,1},{1,0},{2,3},{3,2},{4,5},{5,4},{6,7},{7,6},{8,9},{9,8},{10,11... | collective-permute-start | bytes 4325384 | tf_op jit(solution)/shard_map/ppermute | solution.py:362
  137.5 7.1 %collective-permute-start.33 = (bf16[8,64,640]{2,1,0:T(8,128)(2,1)}, bf16[8,64,640]{2,1,0:T(8,128)(2,1)}, u32[]{:S(2)}, u32[]{:S(2)}) collective-permute-start(bf16[8,64,640]{2,1,0:T(8,128)(2,1)} %collective-permute-done.24.refs_3_), channel_id=1, source_target_pairs={{0,1},{1,0},{2,3},{3,2},{4,5},{5,4},{6,7},{7,6},{8,9},{9,8},{10,11... | collective-permute-start | bytes 1966088 | tf_op jit(solution)/shard_map/ppermute | solution.py:362
  138.0 6.7 %collective-permute-start.34 = (bf16[8,64,640]{2,1,0:T(8,128)(2,1)}, bf16[8,64,640]{2,1,0:T(8,128)(2,1)}, u32[]{:S(2)}, u32[]{:S(2)}) collective-permute-start(bf16[8,64,640]{2,1,0:T(8,128)(2,1)} %get-tuple-element.376.refs_1_), channel_id=1, source_target_pairs={{0,1},{1,0},{2,3},{3,2},{4,5},{5,4},{6,7},{7,6},{8,9},{9,8},{10,11... | collective-permute-start | bytes 1966088 | tf_op jit(solution)/shard_map/ppermute | solution.py:362
  140.9 18.0 %collective-permute-start.30 = (bf16[8,256,384]{2,1,0:T(8,128)(2,1)}, bf16[8,256,384]{2,1,0:T(8,128)(2,1)}, u32[]{:S(2)}, u32[]{:S(2)}) collective-permute-start(bf16[8,256,384]{2,1,0:T(8,128)(2,1)} %get-tuple-element.385.refs_0_), channel_id=1, source_target_pairs={{0,1},{1,0},{2,3},{3,2},{4,5},{5,4},{6,7},{7,6},{8,9},{9,8},{10,11... | collective-permute-start | bytes 4718600 | tf_op jit(solution)/shard_map/ppermute | solution.py:362
  141.4 19.9 %collective-permute-start.28 = (bf16[8,256,384]{2,1,0:T(8,128)(2,1)}, bf16[8,256,384]{2,1,0:T(8,128)(2,1)}, u32[]{:S(2)}, u32[]{:S(2)}) collective-permute-start(bf16[8,256,384]{2,1,0:T(8,128)(2,1)} %get-tuple-element.385.refs_0_), channel_id=1, source_target_pairs={{0,2},{1,5},{2,0},{3,7},{4,6},{5,1},{6,4},{7,3},{8,10},{9,13},{10,... | collective-permute-start | bytes 4718600 | tf_op jit(solution)/shard_map/ppermute | solution.py:362
  144.7 13.4 %collective-permute-start.31 = (bf16[8,256,128]{2,1,0:T(8,128)(2,1)S(1)}, bf16[8,256,128]{2,1,0:T(8,128)(2,1)S(1)}, u32[]{:S(2)}, u32[]{:S(2)}) collective-permute-start(bf16[8,256,128]{2,1,0:T(8,128)(2,1)S(1)} %get-tuple-element.386.refs_1_), channel_id=1, source_target_pairs={{0,1},{1,0},{2,3},{3,2},{4,5},{5,4},{6,7},{7,6},{8,9},{9,8},{10,11... | collective-permute-start | bytes 1572872 | tf_op jit(solution)/shard_map/ppermute | solution.py:362
  144.8 14.1 %collective-permute-start.29 = (bf16[8,256,128]{2,1,0:T(8,128)(2,1)S(1)}, bf16[8,256,128]{2,1,0:T(8,128)(2,1)}, u32[]{:S(2)}, u32[]{:S(2)}) collective-permute-start(bf16[8,256,128]{2,1,0:T(8,128)(2,1)S(1)} %get-tuple-element.386.refs_1_), channel_id=1, source_target_pairs={{0,16},{1,17},{2,18},{3,19},{4,20},{5,21},{6,22},{7,23},{8,24},{9,... | collective-permute-start | bytes 1572872 | tf_op jit(solution)/shard_map/ppermute | solution.py:362
  161.3 5.1 %collective-permute-start.35 = (bf16[8,256,384]{2,1,0:T(8,128)(2,1)}, bf16[8,256,384]{2,1,0:T(8,128)(2,1)}, u32[]{:S(2)}, u32[]{:S(2)}) collective-permute-start(bf16[8,256,384]{2,1,0:T(8,128)(2,1)} %collective-permute-done.28.refs_2_), channel_id=1, source_target_pairs={{0,1},{1,0},{2,3},{3,2},{4,5},{5,4},{6,7},{7,6},{8,9},{9,8},{10,11... | collective-permute-start | bytes 4718600 | tf_op jit(solution)/shard_map/ppermute | solution.py:362
  187.0 8.9 %collective-permute-start.37 = (bf16[32,128,384]{2,1,0:T(8,128)(2,1)}, bf16[32,128,384]{2,1,0:T(8,128)(2,1)}, u32[]{:S(2)}, u32[]{:S(2)}) collective-permute-start(bf16[32,128,384]{2,1,0:T(8,128)(2,1)} %get-tuple-element.396), channel_id=1, source_target_pairs={{0,1},{1,0},{2,3},{3,2},{4,5},{5,4},{6,7},{7,6},{8,9},{9,8},{10,11... | collective-permute-start | bytes 9437192 | tf_op jit(solution)/shard_map/ppermute | solution.py:362
  187.4 8.5 %collective-permute-start.38 = (bf16[32,128,128]{2,1,0:T(8,128)(2,1)}, bf16[32,128,128]{2,1,0:T(8,128)(2,1)}, u32[]{:S(2)}, u32[]{:S(2)}) collective-permute-start(bf16[32,128,128]{2,1,0:T(8,128)(2,1)} %get-tuple-element.397), channel_id=1, source_target_pairs={{0,1},{1,0},{2,3},{3,2},{4,5},{5,4},{6,7},{7,6},{8,9},{9,8},{10,11... | collective-permute-start | bytes 3145736 | tf_op jit(solution)/shard_map/ppermute | solution.py:362
  198.8 13.8 %collective-permute-start.40 = (bf16[16,128,128]{2,1,0:T(8,128)(2,1)S(1)}, bf16[16,128,128]{2,1,0:T(8,128)(2,1)S(1)}, u32[]{:S(2)}, u32[]{:S(2)}) collective-permute-start(bf16[16,128,128]{2,1,0:T(8,128)(2,1)S(1)} %get-tuple-element.409), channel_id=1, source_target_pairs={{0,16},{1,17},{2,18},{3,19},{4,20},{5,21},{6,22},{7,23},{8,24},{9,... | collective-permute-start | bytes 1572872 | tf_op jit(solution)/shard_map/ppermute | solution.py:362
  200.3 19.6 %collective-permute-start.39 = (bf16[16,128,384]{2,1,0:T(8,128)(2,1)S(1)}, bf16[16,128,384]{2,1,0:T(8,128)(2,1)S(1)}, u32[]{:S(2)}, u32[]{:S(2)}) collective-permute-start(bf16[16,128,384]{2,1,0:T(8,128)(2,1)S(1)} %get-tuple-element.408), channel_id=1, source_target_pairs={{0,2},{1,5},{2,0},{3,7},{4,6},{5,1},{6,4},{7,3},{8,10},{9,13},{10,... | collective-permute-start | bytes 4718600 | tf_op jit(solution)/shard_map/ppermute | solution.py:362
  219.8 13.2 %collective-permute-start.43 = (bf16[32,32,1408]{2,1,0:T(8,128)(2,1)S(1)}, bf16[32,32,1408]{2,1,0:T(8,128)(2,1)S(1)}, u32[]{:S(2)}, u32[]{:S(2)}) collective-permute-start(bf16[32,32,1408]{2,1,0:T(8,128)(2,1)S(1)} %get-tuple-element.432), channel_id=1, source_target_pairs={{0,1},{1,0},{2,3},{3,2},{4,5},{5,4},{6,7},{7,6},{8,9},{9,8},{10,11... | collective-permute-start | bytes 8650760 | tf_op jit(solution)/shard_map/ppermute | solution.py:362
  221.3 11.7 %collective-permute-start.44 = (bf16[32,32,640]{2,1,0:T(8,128)(2,1)S(1)}, bf16[32,32,640]{2,1,0:T(8,128)(2,1)S(1)}, u32[]{:S(2)}, u32[]{:S(2)}) collective-permute-start(bf16[32,32,640]{2,1,0:T(8,128)(2,1)S(1)} %get-tuple-element.433), channel_id=1, source_target_pairs={{0,1},{1,0},{2,3},{3,2},{4,5},{5,4},{6,7},{7,6},{8,9},{9,8},{10,11... | collective-permute-start | bytes 3932168 | tf_op jit(solution)/shard_map/ppermute | solution.py:362
  221.9 11.2 %collective-permute-start.41 = (bf16[8,128,384]{2,1,0:T(8,128)(2,1)S(1)}, bf16[8,128,384]{2,1,0:T(8,128)(2,1)S(1)}, u32[]{:S(2)}, u32[]{:S(2)}) collective-permute-start(bf16[8,128,384]{2,1,0:T(8,128)(2,1)S(1)} %get-tuple-element.428), channel_id=1, source_target_pairs={{0,4},{1,17},{2,6},{3,19},{4,0},{5,21},{6,2},{7,23},{8,12},{9,25},... | collective-permute-start | bytes 2359304 | tf_op jit(solution)/shard_map/ppermute | solution.py:362
  222.0 9.9 %collective-permute-start.42 = (bf16[8,128,128]{2,1,0:T(8,128)(2,1)S(1)}, bf16[8,128,128]{2,1,0:T(8,128)(2,1)S(1)}, u32[]{:S(2)}, u32[]{:S(2)}) collective-permute-start(bf16[8,128,128]{2,1,0:T(8,128)(2,1)S(1)} %get-tuple-element.429), channel_id=1, source_target_pairs={{0,2},{1,3},{2,0},{3,1},{4,6},{5,7},{6,4},{7,5},{8,10},{9,11},{10,... | collective-permute-start | bytes 786440 | tf_op jit(solution)/shard_map/ppermute | solution.py:362
  233.4 9.0 %collective-permute-start.46 = (bf16[4,128,128]{2,1,0:T(8,128)(2,1)S(1)}, bf16[4,128,128]{2,1,0:T(8,128)(2,1)S(1)}, u32[]{:S(2)}, u32[]{:S(2)}) collective-permute-start(bf16[4,128,128]{2,1,0:T(8,128)(2,1)S(1)} %get-tuple-element.445), channel_id=1, source_target_pairs={{0,4},{1,5},{2,6},{3,7},{4,0},{5,1},{6,2},{7,3},{8,12},{9,13},{10,... | collective-permute-start | bytes 393224 | tf_op jit(solution)/shard_map/ppermute | solution.py:362
  234.3 8.1 %collective-permute-start.45 = (bf16[4,128,384]{2,1,0:T(8,128)(2,1)S(1)}, bf16[4,128,384]{2,1,0:T(8,128)(2,1)S(1)}, u32[]{:S(2)}, u32[]{:S(2)}) collective-permute-start(bf16[4,128,384]{2,1,0:T(8,128)(2,1)S(1)} %get-tuple-element.444), channel_id=1, source_target_pairs={{0,16},{1,3},{2,18},{3,1},{4,20},{5,7},{6,22},{7,5},{8,24},{9,11},... | collective-permute-start | bytes 1179656 | tf_op jit(solution)/shard_map/ppermute | solution.py:362
  235.4 15.9 %collective-permute-start.48 = (bf16[16,32,640]{2,1,0:T(8,128)(2,1)S(1)}, bf16[16,32,640]{2,1,0:T(8,128)(2,1)S(1)}, u32[]{:S(2)}, u32[]{:S(2)}) collective-permute-start(bf16[16,32,640]{2,1,0:T(8,128)(2,1)S(1)} %get-tuple-element.453), channel_id=1, source_target_pairs={{0,16},{1,17},{2,18},{3,19},{4,20},{5,21},{6,22},{7,23},{8,24},{9,... | collective-permute-start | bytes 1966088 | tf_op jit(solution)/shard_map/ppermute | solution.py:362
  236.9 18.2 %collective-permute-start.47 = (bf16[16,32,1408]{2,1,0:T(8,128)(2,1)S(1)}, bf16[16,32,1408]{2,1,0:T(8,128)(2,1)S(1)}, u32[]{:S(2)}, u32[]{:S(2)}) collective-permute-start(bf16[16,32,1408]{2,1,0:T(8,128)(2,1)S(1)} %get-tuple-element.452), channel_id=1, source_target_pairs={{0,2},{1,5},{2,0},{3,7},{4,6},{5,1},{6,4},{7,3},{8,10},{9,13},{10,... | collective-permute-start | bytes 4325384 | tf_op jit(solution)/shard_map/ppermute | solution.py:362
  255.1 14.0 %collective-permute-start.51 = (bf16[32,32,1536]{2,1,0:T(8,128)(2,1)S(1)}, bf16[32,32,1536]{2,1,0:T(8,128)(2,1)S(1)}, u32[]{:S(2)}, u32[]{:S(2)}) collective-permute-start(bf16[32,32,1536]{2,1,0:T(8,128)(2,1)S(1)} %get-tuple-element.478), channel_id=1, source_target_pairs={{0,1},{1,0},{2,3},{3,2},{4,5},{5,4},{6,7},{7,6},{8,9},{9,8},{10,11... | collective-permute-start | bytes 9437192 | tf_op jit(solution)/shard_map/ppermute | solution.py:362
  258.1 11.0 %collective-permute-start.52 = (bf16[32,32,640]{2,1,0:T(8,128)(2,1)S(1)}, bf16[32,32,640]{2,1,0:T(8,128)(2,1)S(1)}, u32[]{:S(2)}, u32[]{:S(2)}) collective-permute-start(bf16[32,32,640]{2,1,0:T(8,128)(2,1)S(1)} %get-tuple-element.479), channel_id=1, source_target_pairs={{0,1},{1,0},{2,3},{3,2},{4,5},{5,4},{6,7},{7,6},{8,9},{9,8},{10,11... | collective-permute-start | bytes 3932168 | tf_op jit(solution)/shard_map/ppermute | solution.py:362
  258.6 10.5 %collective-permute-start.49 = (bf16[8,32,1408]{2,1,0:T(8,128)(2,1)S(1)}, bf16[8,32,1408]{2,1,0:T(8,128)(2,1)S(1)}, u32[]{:S(2)}, u32[]{:S(2)}) collective-permute-start(bf16[8,32,1408]{2,1,0:T(8,128)(2,1)S(1)} %get-tuple-element.474), channel_id=1, source_target_pairs={{0,4},{1,17},{2,6},{3,19},{4,0},{5,21},{6,2},{7,23},{8,12},{9,25},... | collective-permute-start | bytes 2162696 | tf_op jit(solution)/shard_map/ppermute | solution.py:362
  258.7 7.9 %collective-permute-start.50 = (bf16[8,32,640]{2,1,0:T(8,128)(2,1)S(1)}, bf16[8,32,640]{2,1,0:T(8,128)(2,1)S(1)}, u32[]{:S(2)}, u32[]{:S(2)}) collective-permute-start(bf16[8,32,640]{2,1,0:T(8,128)(2,1)S(1)} %get-tuple-element.475), channel_id=1, source_target_pairs={{0,2},{1,3},{2,0},{3,1},{4,6},{5,7},{6,4},{7,5},{8,10},{9,11},{10,... | collective-permute-start | bytes 983048 | tf_op jit(solution)/shard_map/ppermute | solution.py:362
  270.2 28.5 %collective-permute-start.56 = (bf16[16,32,1536]{2,1,0:T(8,128)(2,1)S(1)}, bf16[16,32,1536]{2,1,0:T(8,128)(2,1)S(1)}, u32[]{:S(2)}, u32[]{:S(2)}) collective-permute-start(bf16[16,32,1536]{2,1,0:T(8,128)(2,1)S(1)} %get-tuple-element.506), channel_id=1, source_target_pairs={{0,2},{1,5},{2,0},{3,7},{4,6},{5,1},{6,4},{7,3},{8,10},{9,13},{10,... | collective-permute-start | bytes 4718600 | tf_op jit(solution)/shard_map/ppermute | solution.py:362
  270.9 27.8 %collective-permute-start.57 = (bf16[16,32,640]{2,1,0:T(8,128)(2,1)S(1)}, bf16[16,32,640]{2,1,0:T(8,128)(2,1)S(1)}, u32[]{:S(2)}, u32[]{:S(2)}) collective-permute-start(bf16[16,32,640]{2,1,0:T(8,128)(2,1)S(1)} %get-tuple-element.507), channel_id=1, source_target_pairs={{0,16},{1,17},{2,18},{3,19},{4,20},{5,21},{6,22},{7,23},{8,24},{9,... | collective-permute-start | bytes 1966088 | tf_op jit(solution)/shard_map/ppermute | solution.py:362
  271.6 27.1 %collective-permute-start.54 = (bf16[4,32,1408]{2,1,0:T(8,128)(2,1)S(1)}, bf16[4,32,1408]{2,1,0:T(8,128)(2,1)S(1)}, u32[]{:S(2)}, u32[]{:S(2)}) collective-permute-start(bf16[4,32,1408]{2,1,0:T(8,128)(2,1)S(1)} %get-tuple-element.498), channel_id=1, source_target_pairs={{0,16},{1,3},{2,18},{3,1},{4,20},{5,7},{6,22},{7,5},{8,24},{9,11},... | collective-permute-start | bytes 1081352 | tf_op jit(solution)/shard_map/ppermute | solution.py:362
  272.2 23.4 %collective-permute-start.53 = (bf16[2,128,512]{2,1,0:T(8,128)(2,1)S(1)}, bf16[2,128,512]{2,1,0:T(8,128)(2,1)S(1)}, u32[]{:S(2)}, u32[]{:S(2)}) collective-permute-start(bf16[2,128,512]{2,1,0:T(8,128)(2,1)S(1)} %pad_maximum_fusion.6), channel_id=1, source_target_pairs={{0,8},{1,9},{2,10},{3,11},{4,12},{5,13},{6,14},{7,15},{8,0},{9,1},... | collective-permute-start | bytes 786440 | tf_op jit(solution)/shard_map/ppermute | solution.py:362
  273.4 25.2 %collective-permute-start.55 = (bf16[4,32,640]{2,1,0:T(8,128)(2,1)S(1)}, bf16[4,32,640]{2,1,0:T(8,128)(2,1)S(1)}, u32[]{:S(2)}, u32[]{:S(2)}) collective-permute-start(bf16[4,32,640]{2,1,0:T(8,128)(2,1)S(1)} %get-tuple-element.499), channel_id=1, source_target_pairs={{0,4},{1,5},{2,6},{3,7},{4,0},{5,1},{6,2},{7,3},{8,12},{9,13},{10,... | collective-permute-start | bytes 491528 | tf_op jit(solution)/shard_map/ppermute | solution.py:362
  300.6 11.3 %collective-permute-start.60 = (bf16[8,32,1536]{2,1,0:T(8,128)(2,1)}, bf16[8,32,1536]{2,1,0:T(8,128)(2,1)S(1)}, u32[]{:S(2)}, u32[]{:S(2)}) collective-permute-start(bf16[8,32,1536]{2,1,0:T(8,128)(2,1)} %get-tuple-element.524), channel_id=1, source_target_pairs={{0,4},{1,17},{2,6},{3,19},{4,0},{5,21},{6,2},{7,23},{8,12},{9,25},... | collective-permute-start | bytes 2359304 | tf_op jit(solution)/shard_map/ppermute | solution.py:362
  301.2 10.0 %collective-permute-start.59 = (bf16[2,32,2048]{2,1,0:T(8,128)(2,1)S(1)}, bf16[2,32,2048]{2,1,0:T(8,128)(2,1)S(1)}, u32[]{:S(2)}, u32[]{:S(2)}) collective-permute-start(bf16[2,32,2048]{2,1,0:T(8,128)(2,1)S(1)} %pad_maximum_fusion.8), channel_id=1, source_target_pairs={{0,8},{1,9},{2,10},{3,11},{4,12},{5,13},{6,14},{7,15},{8,0},{9,1},... | collective-permute-start | bytes 786440 | tf_op jit(solution)/shard_map/ppermute | solution.py:362
  302.2 9.1 %collective-permute-start.61 = (bf16[8,32,640]{2,1,0:T(8,128)(2,1)}, bf16[8,32,640]{2,1,0:T(8,128)(2,1)S(1)}, u32[]{:S(2)}, u32[]{:S(2)}) collective-permute-start(bf16[8,32,640]{2,1,0:T(8,128)(2,1)} %copy-done.26), channel_id=1, source_target_pairs={{0,2},{1,3},{2,0},{3,1},{4,6},{5,7},{6,4},{7,5},{8,10},{9,11},{10,... | collective-permute-start | bytes 983048 | tf_op jit(solution)/shard_map/ppermute | solution.py:362
  312.3 9.9 %collective-permute-start.63 = (bf16[4,32,1536]{2,1,0:T(8,128)(2,1)S(1)}, bf16[4,32,1536]{2,1,0:T(8,128)(2,1)S(1)}, u32[]{:S(2)}, u32[]{:S(2)}) collective-permute-start(bf16[4,32,1536]{2,1,0:T(8,128)(2,1)S(1)} %get-tuple-element.534), channel_id=1, source_target_pairs={{0,16},{1,3},{2,18},{3,1},{4,20},{5,7},{6,22},{7,5},{8,24},{9,11},... | collective-permute-start | bytes 1179656 | tf_op jit(solution)/shard_map/ppermute | solution.py:362
  312.8 5.9 %collective-permute-start.62 = (bf16[32,2048]{1,0:T(8,128)(2,1)S(1)}, bf16[32,2048]{1,0:T(8,128)(2,1)S(1)}, u32[]{:S(2)}, u32[]{:S(2)}) collective-permute-start(bf16[32,2048]{1,0:T(8,128)(2,1)S(1)} %get-tuple-element.585), channel_id=1, source_target_pairs={{0,1},{1,0},{2,3},{3,2},{4,5},{5,4},{6,7},{7,6},{8,9},{9,8},{10,11... | collective-permute-start | bytes 393224 | tf_op jit(solution)/shard_map/ppermute | solution.py:362
  316.4 5.8 %collective-permute-start.64 = (bf16[4,32,640]{2,1,0:T(8,128)(2,1)S(1)}, bf16[4,32,640]{2,1,0:T(8,128)(2,1)S(1)}, u32[]{:S(2)}, u32[]{:S(2)}) collective-permute-start(bf16[4,32,640]{2,1,0:T(8,128)(2,1)S(1)} %get-tuple-element.535), channel_id=1, source_target_pairs={{0,4},{1,5},{2,6},{3,7},{4,0},{5,1},{6,2},{7,3},{8,12},{9,13},{10,... | collective-permute-start | bytes 491528 | tf_op jit(solution)/shard_map/ppermute | solution.py:362
  322.4 14.4 %collective-permute-start.65 = (bf16[2,32,2176]{2,1,0:T(8,128)(2,1)S(1)}, bf16[2,32,2176]{2,1,0:T(8,128)(2,1)S(1)}, u32[]{:S(2)}, u32[]{:S(2)}) collective-permute-start(bf16[2,32,2176]{2,1,0:T(8,128)(2,1)S(1)} %pad_maximum_fusion.4), channel_id=1, source_target_pairs={{0,8},{1,9},{2,10},{3,11},{4,12},{5,13},{6,14},{7,15},{8,0},{9,1},... | collective-permute-start | bytes 835592 | tf_op jit(solution)/shard_map/ppermute | solution.py:362
  324.0 12.8 %collective-permute-start.66 = (bf16[192,1024]{1,0:T(8,128)(2,1)S(1)}, bf16[192,1024]{1,0:T(8,128)(2,1)S(1)}, u32[]{:S(2)}, u32[]{:S(2)}) collective-permute-start(bf16[192,1024]{1,0:T(8,128)(2,1)S(1)} %get-tuple-element.551), channel_id=1, source_target_pairs={{0,16},{16,0},{1,17},{17,1},{2,18},{18,2},{3,19},{19,3},{4,20},{20... | collective-permute-start | bytes 1179656 | tf_op jit(solution)/shard_map/ppermute | solution.py:1106
  (43 other events, 262.2 us)
